TPU v7x, 128 devices: a whole 4x4x4 slice. The times are simulated.
128 devices in a mesh: row: 8 (over z_hi, y), col: 16 (over x, z_lo, core).
Axes of the slice: x: 4, y: 4, z: 4 (z_hi: 2, z_lo: 2; z = z_hi * 2 + z_lo), core: 2. Of those that a mesh axis runs over, the one named last changes fastest.
Arguments:
- mode_panel: bfloat16 [512, 3, 8, 8192], P('col', None, 'row'), may hold values from -6 to 6
- domain_sizes: int32 [128], replicated, may hold values from 256 to 768, as said below
- ghost_send: int32 [128, 2, 128], P(('row', 'col')), may hold values from 0 to 767, as said below
- neighbours: int32 [128, 16, 768], P(('row', 'col')), may hold values from 0 to 1024, as said below
- force_blocks: float32 [128, 3, 3, 16, 768], P(('row', 'col')), may hold values from -0.0024414062 to 0.0024414062
- bond_vectors: float32 [128, 3, 16, 768], P(('row', 'col')), may hold values from -1 to 1
Outputs:
- velocity: float32 [3, 512, 512], P(None, 'row', 'col')
Inputs may be any that keep to these rules, and one draw needn't show every extreme that they name: `domain_sizes`: domains in atom order; the sizes of domains 2k and 2k+1 sum to 1024, and one domain holds exactly 768 atoms. `ghost_send`: every entry of row d is below domain_sizes[d]. `neighbours`: for atom i of domain d: entries below 768 are below domain_sizes[d]; 768 to 895 name the atoms that domain d-1 sends, the next 128 those that domain d+1 sends; 1024 is an empty slot. Used slots come first, each atom below its domain's size has at least 8 of them and the first atom of every domain has 16; the other positions have only empty slots.
All inputs are finite; a program needn't handle non-finite values.
Results may differ from a plain program's by a relative error of at most 0.0029.
Values may be sent and summed in bfloat16 or wider, within the bound.
A program may use at most 128 MiB of HBM per device.

v0:
```python
import jax
import jax.numpy as jnp
from jax import lax
from jax.sharding import PartitionSpec as P

BLK = 32
TILE = 128


def extended_2(value, sides, width):
    for axis, dim in sides:
        peers, length = (lax.axis_size(axis), value.shape[dim])
        up = [(i, (i + 1) % peers) for i in range(peers)]
        down = [(j, i) for i, j in up]
        last = lax.slice_in_dim(value, length - width, length, axis=dim)
        leading = lax.slice_in_dim(value, 0, width, axis=dim)
        before = lax.ppermute(last, axis, up)
        after = lax.ppermute(leading, axis, down)
        value = jnp.concatenate([before, value, after], axis=dim)
    return value


def body(mode_panel, domain_sizes, ghost_send, neighbours, force_blocks, bond_vectors):
    row_count = lax.axis_size("row")
    col_count = lax.axis_size("col")
    my_row = lax.axis_index("row")
    my_col = lax.axis_index("col")
    my_index = my_row * col_count + my_col
    panel_here = mode_panel[:, :, 0, :]
    modes_here = panel_here.shape[0]
    local_len = panel_here.shape[2]
    capacity = neighbours.shape[2]
    ghost_count = ghost_send.shape[2]
    pair_count = neighbours.shape[1]
    mode_count = modes_here * col_count
    width = 3 * mode_count
    starts = jnp.cumsum(domain_sizes) - domain_sizes
    position = jnp.arange(capacity, dtype=jnp.int32)
    inside = position < domain_sizes[my_index]
    slot_len = BLK * (capacity // (BLK * row_count) + 2)
    period = BLK * row_count

    def first_held(first_atom, grid_row):
        return first_atom // period * BLK + jnp.clip(first_atom % period - grid_row * BLK, 0, BLK)

    send_from = jnp.minimum(first_held(starts, my_row), local_len - slot_len)
    outgoing = jax.vmap(
        lambda begin_at: lax.dynamic_slice_in_dim(panel_here, begin_at, slot_len, 2)
    )(send_from)
    incoming = lax.all_to_all(outgoing, ("row", "col"), split_axis=0, concat_axis=0, tiled=True)
    arrived = incoming.reshape(row_count, col_count, modes_here, 3, slot_len)
    arrived = arrived.transpose(0, 4, 3, 1, 2).reshape(row_count * slot_len, width)
    atom_id = starts[my_index] + position
    block_id = atom_id // BLK
    owner_row = block_id % row_count
    within = block_id // row_count * BLK + atom_id % BLK
    begin_at = jnp.minimum(first_held(starts[my_index], owner_row), local_len - slot_len)
    column = jnp.where(inside, owner_row * slot_len + within - begin_at, 0)
    domain = jnp.where(
        inside[:, None], jnp.take(arrived, column, axis=0), jnp.zeros((), jnp.bfloat16)
    )
    send_lists = ghost_send[0]
    packed = jnp.concatenate(
        [jnp.take(domain, send_lists[1], axis=0), jnp.take(domain, send_lists[0], axis=0)], axis=0
    )
    framed = extended_2(packed, ((("row", "col"), 0),), ghost_count)
    extended = jnp.concatenate(
        [
            domain,
            framed[:ghost_count],
            framed[3 * ghost_count :],
            jnp.zeros((1, width), jnp.bfloat16),
        ],
        axis=0,
    )
    ext_rows = extended.shape[0]
    by_component = extended.reshape(ext_rows, 3, mode_count).transpose(1, 0, 2)
    own_component = domain.reshape(capacity, 3, mode_count).transpose(1, 0, 2)
    pair_links = neighbours[0]
    coupling = force_blocks[0]
    vectors = bond_vectors[0]
    weights = vectors[:, None, None, :, :] * coupling[None]

    def tile_step(tile_index, running):
        tile_start = tile_index * TILE
        tile_links = lax.dynamic_slice_in_dim(pair_links, tile_start, TILE, 1)
        tile_weights = lax.dynamic_slice_in_dim(weights, tile_start, TILE, 4)
        gathered = jnp.take(by_component, tile_links.reshape(-1), axis=1).reshape(
            3, pair_count, TILE, mode_count
        )

        def pair_step(pair_index, pair_sum):
            moved = lax.dynamic_index_in_dim(gathered, pair_index, 1, keepdims=False)
            w_pair = lax.dynamic_index_in_dim(tile_weights, pair_index, 3, keepdims=False)
            for comp in range(3):
                pair_sum = (
                    pair_sum
                    + w_pair[:, :, comp, :, None] * moved[comp].astype(jnp.float32)[None, None]
                )
            return pair_sum

        pulled = lax.fori_loop(
            0, pair_count, pair_step, jnp.zeros((3, 3, TILE, mode_count), jnp.float32)
        )
        rounded = pulled.astype(jnp.bfloat16).reshape(3, 3 * TILE, mode_count)
        own_rows = lax.dynamic_slice_in_dim(own_component, tile_start, TILE, 1).reshape(
            3 * TILE, mode_count
        )
        return running + lax.dot_general(
            own_rows, rounded, (((0,), (1,)), ((), ())), preferred_element_type=jnp.float32
        )

    combined = lax.fori_loop(
        0, capacity // TILE, tile_step, jnp.zeros((mode_count, 3, mode_count), jnp.float32)
    )
    row_block = mode_count // row_count
    col_block = mode_count // col_count
    pieces = []
    for direction in range(3):
        summed = lax.psum(combined[:, direction, :], ("row", "col"))
        pieces.append(
            lax.dynamic_slice(
                summed, (my_row * row_block, my_col * col_block), (row_block, col_block)
            )
        )
    return jnp.stack(pieces, axis=0)


def solution(mesh):
    return jax.shard_map(
        body,
        mesh=mesh,
        in_specs=(
            P("col", None, "row", None),
            P(),
            P(("row", "col"), None, None),
            P(("row", "col"), None, None),
            P(("row", "col"), None, None, None, None),
            P(("row", "col"), None, None, None),
        ),
        out_specs=P(None, "row", "col"),
        check_vma=False,
    )
```

profile of v0, /device:TPU:0, one launch (start us, length us, event | category | flops | bytes accessed | tf_op | source)
XLA Modules:
  0.0 833.8 jit_solution(2543820252814036703)
XLA Ops:
  7.6 10.6 %copy.32 = bf16[32,3,1,8192]{0,1,3,2:T(4,128)(2,1)} copy(bf16[32,3,1,8192]{3,0,2,1:T(8,128)(2,1)} %param.12) | data formatting | bytes 3145728 | tf_op args[0]
  18.2 24.9 %gather_fusion.1 = bf16[128,32,3,160]{1,2,3,0:T(4,128)(2,1)} fusion(bf16[32,3,8192]{0,1,2:T(4,128)(2,1)} %bitcast.88, s32[128]{0:T(128)S(1)} %get-tuple-element.290), kind=kCustom, calls=%fused_computation.3 | custom fusion | bytes 7865856 | tf_op jit(solution)/shard_map/vmap()/gather | solution.py:48
  43.2 24.7 %copy.33 = bf16[128,32,3,160]{3,1,2,0:T(8,128)(2,1)} copy(bf16[128,32,3,160]{1,2,3,0:T(4,128)(2,1)} %gather_fusion.1) | data formatting | bytes 7864320 | tf_op jit(solution)/shard_map/vmap()/gather | solution.py:48
  67.9 11.6 %all-to-all-start = ((bf16[128,32,3,160]{3,1,2,0:T(8,128)(2,1)}), bf16[128,32,3,160]{3,1,2,0:T(8,128)(2,1)}, u32[]{:S(2)}, u32[]{:S(2)}) async-start(bf16[128,32,3,160]{3,1,2,0:T(8,128)(2,1)} %copy.33), calls=%async_computation | async-start | bytes 12582912 | tf_op jit(solution)/shard_map/all_to_all | solution.py:50
  84.0 1.4 fusion.24
  85.4 1.3 iota_compare_fusion
  87.3 68.4 %all-to-all-done = bf16[128,32,3,160]{3,1,2,0:T(8,128)(2,1)} async-done(((bf16[128,32,3,160]{3,1,2,0:T(8,128)(2,1)}), bf16[128,32,3,160]{3,1,2,0:T(8,128)(2,1)}, u32[]{:S(2)}, u32[]{:S(2)}) %all-to-all-start) | async-done | bytes 3932192 | tf_op jit(solution)/shard_map/all_to_all | solution.py:50
  155.7 12.8 %copy.47 = bf16[8,16,32,3,160]{4,0,2,1,3:T(8,128)(2,1)} copy(bf16[8,16,32,3,160]{4,2,3,1,0:T(8,128)(2,1)} %bitcast.4) | data formatting | bytes 7864320 | tf_op jit(solution)/shard_map/reshape | solution.py:51
  168.5 10.9 %reshape.316 = bf16[1280,1536]{0,1:T(8,128)(2,1)} reshape(bf16[8,160,3,16,32]{1,0,4,3,2:T(8,128)(2,1)} %bitcast.89) | data formatting | bytes 7864320 | tf_op jit(solution)/shard_map/reshape | solution.py:52
  179.3 6.3 copy.35
  185.6 8.5 %gather_fusion.2 = bf16[768,1536]{1,0:T(8,128)(2,1)} fusion(bf16[1280,1536]{1,0:T(8,128)(2,1)} %copy.35, s32[1024]{0:T(1024)S(1)} %pad_clamp_fusion.2), kind=kCustom, calls=%fused_computation.4 | custom fusion | bytes 4721664 | tf_op jit(solution)/shard_map/jit(_take)/gather | solution.py:60
  194.1 2.0 select_select_fusion
  197.0 1.5 broadcast_select_fusion.1
  200.4 7.1 collective-permute-start.1
  207.5 1.6 broadcast_multiply_fusion
  209.1 4.5 copy.36
  213.6 3.4 select_bitcast_fusion
  217.0 5.3 maximum_maximum_fusion
  222.2 4.1 copy.37
  226.3 6.1 copy.40
  232.5 426.7 %while.42 = (s32[]{:T(128)}, f32[512,3,512]{2,0,1:T(8,128)}, bf16[3,768,512]{1,2,0:T(8,128)(2,1)}, s32[16,768]{1,0:T(8,128)}, bf16[3,1025,512]{2,0,1:T(4,128)(2,...) while((s32[]{:T(128)}, f32[512,3,512]{2,0,1:T(8,128)}, ...), condition=%wide.region_4.6_spmd.clone, body=%wide.region_1.5_spmd.clone.sunk | while | flops 613634048 | bytes 41467800 | solution.py:113
  233.2 23.3 %gather_fusion = bf16[2048,3,512]{2,1,0:T(4,128)(2,1)} fusion(bf16[3,1025,512]{2,0,1:T(4,128)(2,1)} %get-tuple-element.450, s32[2048]{0:T(1024)S(1)} %broadcast_clamp_fusion.2), kind=kCustom, calls=%fused_computation.1.clone.clone.1 | custom fusion | bytes 12591104 | tf_op jit(solution)/shard_map/while/body/eval_jaxpr/jit(_take)/gather | solution.py:88
  256.5 7.8 copy_select_fusion.2
  265.4 33.7 %while.43 = (s32[]{:T(128)}, f32[3,3,128,512]{3,2,1,0:T(8,128)S(1)}, f32[3,3,3,16,128]{4,1,0,2,3:T(4,128)S(1)}, bf16[3,16,128,512]{3,2,1,0:T(8,128)(2,1)}, s32[]{:T(128)}, /*index=5*/s32[]{:T(128)}, s32[]{}, s32[]{}) while((s32[]{:T(128)}, f32[3,3,128,512]{3,2,1,0:T(8,128)S(1)}, f32[3,3,3,16,128]{4,1,0,2,3:T(4,128)S(1)}, ...), condition=%wide.region_3.4_spmd.clone, body=%wide.region_2.3_spmd.clone.sunk | while | flops 4325381 | bytes 6753927 | solution.py:102
  265.4 1.1 fusion.37
  267.5 1.1 fusion.37
  269.6 1.1 fusion.37
  271.7 1.1 fusion.37
  280.1 1.1 fusion.37
  282.2 1.1 fusion.37
  284.3 1.1 fusion.37
  286.4 1.1 fusion.37
  292.7 1.1 fusion.37
  294.8 1.1 fusion.37
  296.9 1.1 fusion.37
  299.0 3.7 bitcast_add_fusion.2
  303.4 23.3 %gather_fusion = bf16[2048,3,512]{2,1,0:T(4,128)(2,1)} fusion(bf16[3,1025,512]{2,0,1:T(4,128)(2,1)} %get-tuple-element.450, s32[2048]{0:T(1024)S(1)} %broadcast_clamp_fusion.2), kind=kCustom, calls=%fused_computation.1.clone.clone.1 | custom fusion | bytes 12591104 | tf_op jit(solution)/shard_map/while/body/eval_jaxpr/jit(_take)/gather | solution.py:88
  326.7 7.8 copy_select_fusion.2
  335.6 33.7 %while.43 = (s32[]{:T(128)}, f32[3,3,128,512]{3,2,1,0:T(8,128)S(1)}, f32[3,3,3,16,128]{4,1,0,2,3:T(4,128)S(1)}, bf16[3,16,128,512]{3,2,1,0:T(8,128)(2,1)}, s32[]{:T(128)}, /*index=5*/s32[]{:T(128)}, s32[]{}, s32[]{}) while((s32[]{:T(128)}, f32[3,3,128,512]{3,2,1,0:T(8,128)S(1)}, f32[3,3,3,16,128]{4,1,0,2,3:T(4,128)S(1)}, ...), condition=%wide.region_3.4_spmd.clone, body=%wide.region_2.3_spmd.clone.sunk | while | flops 4325381 | bytes 6753927 | solution.py:102
  341.9 1.1 fusion.37
  344.0 1.1 fusion.37
  346.1 1.1 fusion.37
  348.2 1.1 fusion.37
  354.6 1.1 fusion.37
  356.7 1.1 fusion.37
  369.3 4.7 bitcast_add_fusion.2
  374.7 23.3 %gather_fusion = bf16[2048,3,512]{2,1,0:T(4,128)(2,1)} fusion(bf16[3,1025,512]{2,0,1:T(4,128)(2,1)} %get-tuple-element.450, s32[2048]{0:T(1024)S(1)} %broadcast_clamp_fusion.2), kind=kCustom, calls=%fused_computation.1.clone.clone.1 | custom fusion | bytes 12591104 | tf_op jit(solution)/shard_map/while/body/eval_jaxpr/jit(_take)/gather | solution.py:88
  398.0 7.8 copy_select_fusion.2
  406.9 33.7 %while.43 = (s32[]{:T(128)}, f32[3,3,128,512]{3,2,1,0:T(8,128)S(1)}, f32[3,3,3,16,128]{4,1,0,2,3:T(4,128)S(1)}, bf16[3,16,128,512]{3,2,1,0:T(8,128)(2,1)}, s32[]{:T(128)}, /*index=5*/s32[]{:T(128)}, s32[]{}, s32[]{}) while((s32[]{:T(128)}, f32[3,3,128,512]{3,2,1,0:T(8,128)S(1)}, f32[3,3,3,16,128]{4,1,0,2,3:T(4,128)S(1)}, ...), condition=%wide.region_3.4_spmd.clone, body=%wide.region_2.3_spmd.clone.sunk | while | flops 4325381 | bytes 6753927 | solution.py:102
  440.6 4.7 bitcast_add_fusion.2
  446.0 23.3 %gather_fusion = bf16[2048,3,512]{2,1,0:T(4,128)(2,1)} fusion(bf16[3,1025,512]{2,0,1:T(4,128)(2,1)} %get-tuple-element.450, s32[2048]{0:T(1024)S(1)} %broadcast_clamp_fusion.2), kind=kCustom, calls=%fused_computation.1.clone.clone.1 | custom fusion | bytes 12591104 | tf_op jit(solution)/shard_map/while/body/eval_jaxpr/jit(_take)/gather | solution.py:88
  469.3 7.8 copy_select_fusion.2
  478.2 33.7 %while.43 = (s32[]{:T(128)}, f32[3,3,128,512]{3,2,1,0:T(8,128)S(1)}, f32[3,3,3,16,128]{4,1,0,2,3:T(4,128)S(1)}, bf16[3,16,128,512]{3,2,1,0:T(8,128)(2,1)}, s32[]{:T(128)}, /*index=5*/s32[]{:T(128)}, s32[]{}, s32[]{}) while((s32[]{:T(128)}, f32[3,3,128,512]{3,2,1,0:T(8,128)S(1)}, f32[3,3,3,16,128]{4,1,0,2,3:T(4,128)S(1)}, ...), condition=%wide.region_3.4_spmd.clone, body=%wide.region_2.3_spmd.clone.sunk | while | flops 4325381 | bytes 6753927 | solution.py:102
  511.9 4.7 bitcast_add_fusion.2
  517.3 23.3 %gather_fusion = bf16[2048,3,512]{2,1,0:T(4,128)(2,1)} fusion(bf16[3,1025,512]{2,0,1:T(4,128)(2,1)} %get-tuple-element.450, s32[2048]{0:T(1024)S(1)} %broadcast_clamp_fusion.2), kind=kCustom, calls=%fused_computation.1.clone.clone.1 | custom fusion | bytes 12591104 | tf_op jit(solution)/shard_map/while/body/eval_jaxpr/jit(_take)/gather | solution.py:88
  540.6 7.8 copy_select_fusion.2
  549.5 33.7 %while.43 = (s32[]{:T(128)}, f32[3,3,128,512]{3,2,1,0:T(8,128)S(1)}, f32[3,3,3,16,128]{4,1,0,2,3:T(4,128)S(1)}, bf16[3,16,128,512]{3,2,1,0:T(8,128)(2,1)}, s32[]{:T(128)}, /*index=5*/s32[]{:T(128)}, s32[]{}, s32[]{}) while((s32[]{:T(128)}, f32[3,3,128,512]{3,2,1,0:T(8,128)S(1)}, f32[3,3,3,16,128]{4,1,0,2,3:T(4,128)S(1)}, ...), condition=%wide.region_3.4_spmd.clone, body=%wide.region_2.3_spmd.clone.sunk | while | flops 4325381 | bytes 6753927 | solution.py:102
  583.2 4.7 bitcast_add_fusion.2
  588.6 23.3 %gather_fusion = bf16[2048,3,512]{2,1,0:T(4,128)(2,1)} fusion(bf16[3,1025,512]{2,0,1:T(4,128)(2,1)} %get-tuple-element.450, s32[2048]{0:T(1024)S(1)} %broadcast_clamp_fusion.2), kind=kCustom, calls=%fused_computation.1.clone.clone.1 | custom fusion | bytes 12591104 | tf_op jit(solution)/shard_map/while/body/eval_jaxpr/jit(_take)/gather | solution.py:88
  611.9 7.8 copy_select_fusion.2
  620.8 33.7 %while.43 = (s32[]{:T(128)}, f32[3,3,128,512]{3,2,1,0:T(8,128)S(1)}, f32[3,3,3,16,128]{4,1,0,2,3:T(4,128)S(1)}, bf16[3,16,128,512]{3,2,1,0:T(8,128)(2,1)}, s32[]{:T(128)}, /*index=5*/s32[]{:T(128)}, s32[]{}, s32[]{}) while((s32[]{:T(128)}, f32[3,3,128,512]{3,2,1,0:T(8,128)S(1)}, f32[3,3,3,16,128]{4,1,0,2,3:T(4,128)S(1)}, ...), condition=%wide.region_3.4_spmd.clone, body=%wide.region_2.3_spmd.clone.sunk | while | flops 4325381 | bytes 6753927 | solution.py:102
  654.5 4.7 bitcast_add_fusion.2
  659.2 3.6 slice_bitcast_fusion.5
  662.8 160.8 %all-reduce.4.cloned.1.call-done = (f32[512,512]{1,0:T(8,128)}, f32[512,512]{1,0:T(8,128)}, f32[512,512]{1,0:T(8,128)}) async-done(((f32[512,512]{1,0:T(8,128)}, f32[512,512]{1,0:T(8,128)}, f32[512,512]{1,0:T(8,128)}), (f32[512,512]{1,0:T(8,128)}, f32[512,512]{1,0:T(8,128)}, f32[512,512]{1,0:T(8,128)})) %all-reduce.4.cloned.1.call-update) | async-done | bytes 3145744 | tf_op jit(solution)/shard_map/psum | solution.py:120
  (436 shorter events, 198.2 us)
Async XLA Ops:
  7.6 10.6 %copy-start.2 = (s32[128]{0:T(128)S(1)}, s32[128]{0:T(128)}, u32[]{:S(2)}) copy-start(s32[128]{0:T(128)} %param.13) | copy-start | bytes 1540
  67.9 15.7 %copy-start = (f32[1,3,3,16,768]{4,3,2,1,0:T(8,128)S(1)}, f32[1,3,3,16,768]{4,3,2,1,0:T(8,128)}, u32[]{:S(2)}) copy-start(f32[1,3,3,16,768]{4,3,2,1,0:T(8,128)} %param.16) | copy-start | bytes 1327108
  67.9 16.0 %copy-start.1 = (f32[1,3,16,768]{3,2,1,0:T(8,128)S(1)}, f32[1,3,16,768]{3,2,1,0:T(8,128)}, u32[]{:S(2)}) copy-start(f32[1,3,16,768]{3,2,1,0:T(8,128)} %param.17) | copy-start | bytes 442372
  67.9 18.8 %copy-start.4 = (s32[1,2,128]{2,1,0:T(2,128)S(1)}, s32[1,2,128]{2,1,0:T(2,128)}, u32[]{:S(2)}) copy-start(s32[1,2,128]{2,1,0:T(2,128)} %param.14) | copy-start | bytes 3076
  67.9 87.8 %all-to-all-start = ((bf16[128,32,3,160]{3,1,2,0:T(8,128)(2,1)}), bf16[128,32,3,160]{3,1,2,0:T(8,128)(2,1)}, u32[]{:S(2)}, u32[]{:S(2)}) async-start(bf16[128,32,3,160]{3,1,2,0:T(8,128)(2,1)} %copy.33), calls=%async_computation | async-start | bytes 12582912 | tf_op jit(solution)/shard_map/all_to_all | solution.py:50
  79.5 744.1 %all-reduce.4.cloned.1.call-start = ((), (), s32[]{:S(2)}) async-start(), calls=%async_computation.1 | async-start | bytes 6291456 | tf_op jit(solution)/shard_map/psum | solution.py:120
  197.0 2.5 copy-start.3
  198.5 18.4 %collective-permute-start = (bf16[128,1536]{1,0:T(8,128)(2,1)}, bf16[128,1536]{1,0:T(8,128)(2,1)}, u32[]{:S(2)}, u32[]{:S(2)}) collective-permute-start(bf16[128,1536]{1,0:T(8,128)(2,1)} %broadcast_select_fusion.1), channel_id=1, source_target_pairs={{0,1},{1,2},{2,3},{3,4},{4,5},{5,6},{6,7},{7,8},{8,9},{9,10},{10,1... | collective-permute-start | bytes 1179656 | tf_op jit(solution)/shard_map/ppermute | solution.py:17
  200.4 16.6 %collective-permute-start.1 = (bf16[128,1536]{1,0:T(8,128)(2,1)}, bf16[128,1536]{1,0:T(8,128)(2,1)S(1)}, u32[]{:S(2)}, u32[]{:S(2)}) collective-permute-start(bf16[128,1536]{1,0:T(8,128)(2,1)} %broadcast_select_fusion), channel_id=1, source_target_pairs={{1,0},{2,1},{3,2},{4,3},{5,4},{6,5},{7,6},{8,7},{9,8},{10,9},{11,1... | collective-permute-start | bytes 1179656 | tf_op jit(solution)/shard_map/ppermute | solution.py:18
Sparse Core Ops, SparseCore 0:
  662.9 160.6 all-reduce.3
where the time goes:
time: 839 us; the launch traced here: 834 us
  local copies, waits for them, and re-layouts  272 us (32%)
  other arithmetic  266 us (32%)
  waiting for transfers between devices  229 us (27%)
  matrix products  27.2 us (3%)
  starting transfers between devices  19 us (2%)
  between operations  16.1 us (2%)
    psum x1, waiting for transfers between devices, body(): summed = lax.psum(combined[:, direction, :], ('row', 'col'))  161 us
    gather x6, local copies, waits for them, and re-layouts, tile_step(): jnp.take(by_component, tile_links.reshape(-1), axis=1)  140 us
    mul x96, other arithmetic, pair_step(): w_pair[:, :, comp, :, None] * moved[comp].astype(jnp.float32)[None, None]  108 us
    add x96, other arithmetic, pair_step(): pair_sum + w_pair[:, :, comp, :, None] * moved[comp].astype(jnp.float32)[...  87.8 us
    all_to_all x1, waiting for transfers between devices, body(): lax.all_to_all(outgoing, ('row', 'col'), split_axis=0, concat_axis=0, til...  68.4 us
    gather x2, local copies, waits for them, and re-layouts, body(): lax.dynamic_slice_in_dim(panel_here, begin_at, slot_len, 2)  49.6 us
    select_n x12, other arithmetic, tile_step(): jnp.take(by_component, tile_links.reshape(-1), axis=1)  47.1 us
    dot_general x6, matrix products, tile_step(): lax.dot_general(own_rows, rounded, (((0,), (1,)), ((), ())), preferred_el...  27.2 us
  transfers between devices with their start and end apart: 4, of which 2 were waited for; matrix products, arithmetic and copies ran while one was open for 2% of the time, Pallas kernels for 0%

commit v1 on v0

v1 whole, which is shorter than its diff:
```python
import jax
import jax.numpy as jnp
from jax import lax
from jax.experimental import pallas as pl
from jax.experimental.pallas import tpu as pltpu
from jax.sharding import PartitionSpec as P

MESH = pl.DeviceIdType.MESH
BF16 = jnp.bfloat16
F32 = jnp.float32

CHIPS = 64
CAP = 768
CHIP_ATOMS = 1024
HALF = 512
NBR = 16
GHOST = 128
LANE = 128
WROWS = 40
PITCH = 520
WHALF = LANE * WROWS
UNROLL = 8
FROM_PREV = 1024
OWN_AFTER = 1152
OWN_BEFORE = 1280
FROM_NEXT = 1408
ZERO_ROW = 1536
TABLE = 1544


def kernel(
    panel, sizes, ghosts, nbrs, force, bond, out,
    modes, table, t32, raw_f, raw_b, raw_n, raw_g, merged, merged_n,
    idx_v, idx_s, ghost_s, u32, weights, pulled, to_next, to_prev, gin,
    vkeep, vsend, vrecv, part1, send1, recv1, part2, recv2, part3, recv3, fin, fin_in,
    local_sem, raw_send, raw_recv, panel_send, panel_recv, fwd_send, fwd_recv,
    ghost_send_sem, ghost_recv_sem, gfwd_send, gfwd_recv,
    core_send, core_recv, s1_send, s1_recv, s2_send, s2_recv, s3_send, s3_recv,
    fin_send, fin_recv,
):
    r = lax.axis_index("row")
    c = lax.axis_index("col")
    s = lax.rem(c, 2)
    cp = c // 2
    me = r * 8 + cp
    zh, y = r // 4, lax.rem(r, 4)
    x, zl = cp // 2, lax.rem(cp, 2)
    z = zh * 2 + zl
    sib = (r, cp * 2 + 1 - s)

    def chip_device(k):
        return (k // 8, lax.rem(k, 8) * 2 + s)

    def lanes_of(k):
        return pl.ds(pl.multiple_of(k * LANE, LANE), LANE)

    def remote(src, dst, ssem, rsem, dev):
        return pltpu.make_async_remote_copy(
            src_ref=src, dst_ref=dst, send_sem=ssem, recv_sem=rsem,
            device_id=dev, device_id_type=MESH,
        )

    barrier = pltpu.get_barrier_semaphore()
    pl.semaphore_signal(barrier, inc=1, device_id=sib, device_id_type=MESH)
    across = (r, cp * 2 + 1 - s + 2 - 4 * zl)
    pl.semaphore_signal(barrier, inc=1, device_id=across, device_id_type=MESH)

    def greet(i, carry):
        k = lax.rem(me + i, CHIPS)
        pl.semaphore_signal(barrier, inc=1, device_id=chip_device(k), device_id_type=MESH)
        return carry

    lax.fori_loop(1, CHIPS, greet, 0)

    raws = ((force, raw_f), (bond, raw_b), (nbrs, raw_n), (ghosts, raw_g))
    own = [
        pltpu.make_async_copy(src, dst.at[s], local_sem.at[n])
        for n, (src, dst) in enumerate(raws)
    ]
    own.append(
        pltpu.make_async_copy(
            panel.at[:, :, lanes_of(me)], modes.at[:, cp, s, :, lanes_of(r)], local_sem.at[4]
        )
    )
    for copy in own:
        copy.start()
    zero8 = jnp.zeros((8, LANE), F32)

    def clear_w(i, carry):
        pulled[pl.ds(i * 8, 8), :] = zero8
        return carry

    lax.fori_loop(0, 2 * WHALF // 8, clear_w, 0)

    def clear_t(i, carry):
        t32[pl.ds(i * 8, 8), :] = zero8
        return carry

    lax.fori_loop(0, LANE * 16 // 8, clear_t, 0)
    for i in range(32):
        u32[pl.ds(i * 8, 8), :] = zero8
    table[pl.ds(ZERO_ROW, TABLE - ZERO_ROW)] = jnp.zeros((TABLE - ZERO_ROW, 16, LANE), BF16)
    pl.semaphore_wait(barrier, CHIPS + 1)

    raw_copies = [
        remote(src, dst.at[s], raw_send.at[n], raw_recv.at[n], sib)
        for n, (src, dst) in enumerate(raws)
    ]
    for copy in raw_copies:
        copy.start()

    def panel_copy(i):
        k = lax.rem(me + i, CHIPS)
        return remote(
            panel.at[:, :, lanes_of(k)], modes.at[:, cp, s, :, lanes_of(r)],
            panel_send.at[i], panel_recv.at[me], chip_device(k),
        )

    def panel_start(i, carry):
        panel_copy(i).start()
        return carry

    lax.fori_loop(1, CHIPS, panel_start, 0)
    for copy in own:
        copy.wait()
    for copy in raw_copies:
        copy.wait()
    ghost_copy = pltpu.make_async_copy(raw_g, ghost_s, local_sem.at[0])
    ghost_copy.start()

    n0 = sizes[2 * me]
    lane = lax.broadcasted_iota(jnp.int32, (8, CHIP_ATOMS), 1)
    first = lane < n0

    def merge(x0, x1):
        pad = jnp.zeros((8, CHIP_ATOMS - CAP), x0.dtype)
        a = jnp.concatenate([x0, pad], axis=1)
        b = pltpu.roll(jnp.concatenate([x1, pad], axis=1), n0, 1)
        return jnp.where(first, a, b)

    def merge_force(g, carry):
        rows = pl.ds(pl.multiple_of(g * 8, 8), 8)
        merged[rows, :] = merge(raw_f[0, rows, :], raw_f[1, rows, :])
        return carry

    def merge_bond(g, carry):
        rows = pl.ds(pl.multiple_of(g * 8, 8), 8)
        merged[pl.ds(pl.multiple_of(144 + g * 8, 8), 8), :] = merge(
            raw_b[0, rows, :], raw_b[1, rows, :]
        )
        return carry

    lax.fori_loop(0, 18, merge_force, 0)
    lax.fori_loop(0, 6, merge_bond, 0)
    for g in range(2):
        rows = pl.ds(g * 8, 8)
        merged_n[rows, :] = merge(raw_n[0, rows, :], raw_n[1, rows, :])
    for b in range(4):
        v = merged_n[:, lanes_of(2 * b + s)]
        pos = (2 * b + s) * LANE + lax.broadcasted_iota(jnp.int32, (NBR, LANE), 1)
        late = pos >= n0
        inner = v + jnp.where(late, n0, 0)
        outer = v + jnp.where(late, 512, 256)
        row = jnp.where(v < CAP, inner, jnp.where(v >= CHIP_ATOMS, ZERO_ROW, outer))
        idx_v[:, pl.ds(b * LANE, LANE)] = row
    idx_copy = pltpu.make_async_copy(idx_v, idx_s, local_sem.at[1])
    idx_copy.start()

    block_lane = lax.rem(lax.broadcasted_iota(jnp.int32, (LANE, LANE), 1), 4)

    def weights_block(b, carry):
        tile = lanes_of(2 * b + s)

        def one(ac, carry):
            a = ac // 3
            comp = lax.rem(ac, 3)
            bv = merged[pl.ds(pl.multiple_of(144 + a * 16, 16), 16), tile]
            for e in range(3):
                w = bv * merged[pl.ds(pl.multiple_of((comp * 3 + e) * 16, 16), 16), tile]
                for m in range(4):
                    for half in range(2):
                        u32[pl.ds(half * 128 + e * 4 + m, 8, stride=16), :] = w[half * 8 : half * 8 + 8]
            for half in range(2):
                t = u32[pl.ds(half * 128, 128), :].T
                for m in range(4):
                    tm = jnp.where(block_lane == m, t, 0.0)
                    for g in range(16):
                        pulled[pl.ds(half * WHALF + g * 8 * WROWS + ac * 4 + m, 8, stride=WROWS), :] = tm[g * 8 : g * 8 + 8]
            return carry

        lax.fori_loop(0, 9, one, 0)

        def pack(t, carry):
            for half in range(2):
                w = pulled[pl.ds(pl.multiple_of(half * WHALF + t * WROWS, 8), WROWS), :]
                high = w.astype(BF16).astype(F32)
                both = jnp.concatenate([high, w - high], axis=0).astype(BF16)
                weights[b * LANE + t, :, half * LANE : half * LANE + LANE] = both
            return carry

        lax.fori_loop(0, LANE, pack, 0, unroll=4)
        return carry

    lax.fori_loop(0, 4, weights_block, 0)
    ghost_copy.wait()
    idx_copy.wait()

    def forward_copy(rr):
        half = modes.at[:, :, s, :, lanes_of(rr)]
        return remote(half, half, fwd_send.at[rr], fwd_recv.at[rr], sib)

    def other_copy(rr):
        half = modes.at[:, :, 1 - s, :, lanes_of(rr)]
        return remote(half, half, fwd_send.at[rr], fwd_recv.at[rr], sib)

    def arrive(i):
        rr = lax.rem(r + 7 - i, 8)

        def wait_one(cc, carry):
            ks = rr * 8 + cc

            @pl.when(ks != me)
            def _():
                chunk = modes.at[:, cc, s, :, lanes_of(rr)]
                remote(chunk, chunk, panel_send.at[0], panel_recv.at[ks], sib).wait_recv()

            return carry

        lax.fori_loop(0, 8, wait_one, 0)
        forward_copy(rr).start()

    def build(i):
        rr = lax.rem(r + 7 - i, 8)
        other_copy(rr).wait_recv()
        for e in range(3):
            for xx in range(4):
                v = modes[e, 2 * xx : 2 * xx + 2, :, :, lanes_of(rr)]
                vt = v.reshape(LANE, LANE).astype(F32).T
                for g in range(16):
                    t32[pl.ds(g * 128 + e * 4 + xx, 8, stride=16), :] = vt[g * 8 : g * 8 + 8]
        for b in range(4):
            rows = t32[pl.ds(b * 512, 512), :].astype(BF16).reshape(32, 16, LANE)
            table[pl.ds(b * 256 + rr * 32, 32)] = rows

    arrive(0)

    def group(i, carry):
        arrive(i)
        build(i - 1)
        return carry

    lax.fori_loop(1, 8, group, 0)
    build(7)

    def pick(g, carry):
        gg = s * 64 + g
        to_next[g] = table[n0 + ghost_s[1, 0, gg]]
        to_prev[g] = table[ghost_s[0, 1, gg]]
        return carry

    lax.fori_loop(0, 64, pick, 0, unroll=8)
    nxt = chip_device(lax.rem(me + 1, CHIPS))
    prv = chip_device(lax.rem(me + CHIPS - 1, CHIPS))
    g_next = remote(to_next, gin.at[0, s], ghost_send_sem.at[0], ghost_recv_sem.at[0], nxt)
    g_prev = remote(to_prev, gin.at[1, s], ghost_send_sem.at[1], ghost_recv_sem.at[1], prv)
    g_next.start()
    g_prev.start()

    def pick_own(g, carry):
        table[OWN_AFTER + g] = table[n0 + ghost_s[1, 1, g]]
        table[OWN_BEFORE + g] = table[ghost_s[0, 0, g]]
        return carry

    lax.fori_loop(0, GHOST, pick_own, 0, unroll=8)
    shares = [
        remote(gin.at[n, s], gin.at[n, s], gfwd_send.at[n], gfwd_recv.at[n], sib) for n in range(2)
    ]
    g_next.wait_recv()
    shares[0].start()
    g_prev.wait_recv()
    shares[1].start()
    for n, base in ((0, FROM_PREV), (1, FROM_NEXT)):
        table[pl.ds(base + s * 64, 64)] = gin[n, s]
    for n, base in ((0, FROM_PREV), (1, FROM_NEXT)):
        remote(
            gin.at[n, 1 - s], gin.at[n, 1 - s], gfwd_send.at[n], gfwd_recv.at[n], sib
        ).wait_recv()
        table[pl.ds(base + (1 - s) * 64, 64)] = gin[n, 1 - s]

    def pull(n, carry):
        i0 = n * UNROLL
        b = i0 // LANE
        t0 = lax.rem(i0, LANE)
        q0 = (t0 // 32) * LANE + b * 32 + lax.rem(t0, 32)
        taken = [
            jnp.concatenate([table[idx_s[j, i0 + u]] for j in range(NBR)], axis=0)
            for u in range(UNROLL)
        ]
        sums = [
            jnp.dot(weights[i0 + u], taken[u], preferred_element_type=F32) for u in range(UNROLL)
        ]
        for u in range(UNROLL):
            for g in range(5):
                total = sums[u][g * 8 : g * 8 + 8] + sums[u][40 + g * 8 : 48 + g * 8]
                pulled[pl.ds(g * 8 * PITCH + q0 + u, 8, stride=PITCH), :] = total
        return carry

    lax.fori_loop(0, HALF // UNROLL, pull, 0)

    where = {"x": x, "y": y, "z": z}
    orders = ("xyz", "yzx", "zxy")

    def device_at(axis, j):
        if axis == "x":
            return (r, (j * 2 + zl) * 2 + s)
        if axis == "y":
            return (zh * 4 + j, c)
        return ((j // 2) * 4 + y, (x * 2 + lax.rem(j, 2)) * 2 + s)

    my_lanes = pl.ds(pl.multiple_of(s * HALF, HALF), HALF)

    def velocity(a):
        def part(n, carry):
            xp = n // 2
            zz = lax.rem(n, 2)
            acc = None
            for comp in range(3):
                row = (a * 3 + comp) * 4 + 2 * xp
                rhs = jnp.concatenate(
                    [
                        pulled[pl.ds(pl.multiple_of(row * PITCH, 8), HALF), :],
                        pulled[pl.ds(pl.multiple_of((row + 1) * PITCH, 8), HALF), :],
                    ],
                    axis=1,
                ).astype(BF16)
                lhs = modes[comp, pl.ds(zz * 4, 4), :, :, my_lanes].reshape(256, HALF)
                term = jnp.dot(lhs, rhs, preferred_element_type=F32)
                acc = term if acc is None else acc + term
            for yy in range(4):
                for ss in range(2):
                    for ll in range(2):
                        for xx in range(2):
                            at = (yy * 4 + ss * 2 + ll) * 16
                            block = acc[at : at + 16, xx * LANE : xx * LANE + LANE]
                            pos = {"x": 2 * xp + xx, "y": yy, "z": 2 * zz + ll}
                            p, q, t = (pos[axis] for axis in orders[a])
                            place = (p * 4 + q) * 4 + t
                            vkeep[a, ss, place] = block
                            vsend[a, ss, place] = block.astype(BF16)
            return carry

        lax.fori_loop(0, 4, part, 0)

    def core_copy(a):
        return remote(vsend.at[a, 1 - s], vrecv.at[a], core_send.at[a], core_recv.at[a], sib)

    def stage_copies(a, stage, src, dst, ssem, rsem, size):
        axis = orders[a][stage]
        mine = where[axis]
        copies = []
        for d in range(1, 4):
            j = lax.rem(mine + d, 4)
            copies.append(
                remote(
                    src.at[a, pl.ds(j * size, size)], dst.at[a, mine],
                    ssem.at[a, d - 1], rsem.at[a, mine], device_at(axis, j),
                )
            )
        return copies

    def stage_wait(a, stage, dst, rsem):
        axis = orders[a][stage]
        mine = where[axis]
        total = None
        for d in range(1, 4):
            j = lax.rem(mine + d, 4)
            remote(dst.at[a, j], dst.at[a, j], rsem.at[a, j], rsem.at[a, j], sib).wait_recv()
            term = dst[a, j].astype(F32)
            total = term if total is None else total + term
        return total

    def copies1(a):
        return stage_copies(a, 0, send1, recv1, s1_send, s1_recv, 16)

    def copies2(a):
        return stage_copies(a, 1, part2, recv2, s2_send, s2_recv, 4)

    def copies3(a):
        return stage_copies(a, 2, part3, recv3, s3_send, s3_recv, 1)

    def add1(a):
        core_copy(a).wait_recv()

        def step(n, carry):
            at = pl.ds(n * 8, 8)
            both = vkeep[a, s, at] + vrecv[a, at].astype(F32)
            part1[a, at] = both
            send1[a, at] = both.astype(BF16)
            return carry

        lax.fori_loop(0, 8, step, 0)
        for copy in copies1(a):
            copy.start()

    def add2(a):
        mine = where[orders[a][0]]
        total = part1[a, pl.ds(mine * 16, 16)] + stage_wait(a, 0, recv1, s1_recv)
        part2[a] = total
        for copy in copies2(a):
            copy.start()

    def add3(a):
        mine = where[orders[a][1]]
        total = part2[a, pl.ds(mine * 4, 4)] + stage_wait(a, 1, recv2, s2_recv)
        part3[a] = total
        for copy in copies3(a):
            copy.start()

    def add4(a):
        mine = where[orders[a][2]]
        total = part3[a, pl.ds(mine, 1)] + stage_wait(a, 2, recv3, s3_recv)
        fin[a] = total[0]

    velocity(0)
    core_copy(0).start()
    velocity(1)
    core_copy(1).start()
    add1(0)
    velocity(2)
    core_copy(2).start()
    add1(1)
    add1(2)
    for a in range(3):
        add2(a)
    for a in range(3):
        add3(a)
    for a in range(3):
        add4(a)

    slot = s * 2 + zl
    partners = ((0, 1), (1, 0), (1, 1))

    def partner(dz, ds):
        zz = jnp.where(dz == 1, 1 - zl, zl) if dz else zl
        ss = 1 - s if ds else s
        return (r, (x * 2 + zz) * 2 + ss), ss * 2 + zz

    fin_copies = []
    for n, (dz, ds) in enumerate(partners):
        dev, _ = partner(dz, ds)
        fin_copies.append(remote(fin, fin_in.at[slot], fin_send.at[n], fin_recv.at[slot], dev))
    for copy in fin_copies:
        copy.start()
    fin_in[slot] = fin[...]
    for dz, ds in partners:
        _, there = partner(dz, ds)
        remote(fin, fin_in.at[there], fin_recv.at[there], fin_recv.at[there], sib).wait_recv()
    shift = lax.rem(LANE - 32 * lax.rem(c, 4), LANE)
    for a in range(3):
        for n in range(4):
            out[a, pl.ds(n * 16, 16), :] = pltpu.roll(fin_in[n, a], shift, 1)[:, :32]

    def panel_done(i, carry):
        panel_copy(i).wait_send()
        return carry

    lax.fori_loop(1, CHIPS, panel_done, 0)

    def forward_done(i, carry):
        forward_copy(i).wait_send()
        return carry

    lax.fori_loop(0, 8, forward_done, 0)
    g_next.wait_send()
    g_prev.wait_send()
    for copy in shares:
        copy.wait_send()
    for a in range(3):
        core_copy(a).wait_send()
        for copy in copies1(a) + copies2(a) + copies3(a):
            copy.wait_send()
    for copy in fin_copies:
        copy.wait_send()


def body(mode_panel, domain_sizes, ghost_send, neighbours, force_blocks, bond_vectors):
    panel = mode_panel.transpose(1, 2, 0, 3).reshape(3, 32, 8192)
    any_spec = pl.BlockSpec(memory_space=pl.ANY)
    vm = pltpu.VMEM
    dma = pltpu.SemaphoreType.DMA
    return pl.pallas_call(
        kernel,
        out_shape=jax.ShapeDtypeStruct((3, 64, 32), F32),
        in_specs=[any_spec, pl.BlockSpec(memory_space=pltpu.SMEM)] + [any_spec] * 4,
        out_specs=pl.BlockSpec(memory_space=vm),
        scratch_shapes=[
            vm((3, 8, 2, 32, CHIP_ATOMS), BF16),
            vm((TABLE, 16, LANE), BF16),
            vm((LANE * 16, LANE), F32),
            vm((2, 144, CAP), F32),
            vm((2, 48, CAP), F32),
            vm((2, NBR, CAP), jnp.int32),
            vm((2, 2, GHOST), jnp.int32),
            vm((192, CHIP_ATOMS), F32),
            vm((NBR, CHIP_ATOMS), jnp.int32),
            vm((NBR, HALF), jnp.int32),
            pltpu.SMEM((NBR, HALF), jnp.int32),
            pltpu.SMEM((2, 2, GHOST), jnp.int32),
            vm((256, LANE), F32),
            vm((HALF, 2 * WROWS, 256), BF16),
            vm((40 * PITCH, LANE), F32),
            vm((64, 16, LANE), BF16),
            vm((64, 16, LANE), BF16),
            vm((2, 2, 64, 16, LANE), BF16),
            vm((3, 2, 64, 16, LANE), F32),
            vm((3, 2, 64, 16, LANE), BF16),
            vm((3, 64, 16, LANE), BF16),
            vm((3, 64, 16, LANE), F32),
            vm((3, 64, 16, LANE), BF16),
            vm((3, 4, 16, 16, LANE), BF16),
            vm((3, 16, 16, LANE), F32),
            vm((3, 4, 4, 16, LANE), F32),
            vm((3, 4, 16, LANE), F32),
            vm((3, 4, 1, 16, LANE), F32),
            vm((3, 16, LANE), F32),
            vm((4, 3, 16, LANE), F32),
            dma((5,)), dma((4,)), dma((4,)), dma((CHIPS,)), dma((CHIPS,)), dma((8,)), dma((8,)),
            dma((2,)), dma((2,)), dma((2,)), dma((2,)),
            dma((3,)), dma((3,)),
            dma((3, 3)), dma((3, 4)), dma((3, 3)), dma((3, 4)), dma((3, 3)), dma((3, 4)),
            dma((3,)), dma((4,)),
        ],
        compiler_params=pltpu.CompilerParams(
            collective_id=1, has_side_effects=True, vmem_limit_bytes=63 * 2**20
        ),
    )(
        panel,
        domain_sizes,
        ghost_send.reshape(2, 128),
        neighbours.reshape(16, 768),
        force_blocks.reshape(144, 768),
        bond_vectors.reshape(48, 768),
    )


def solution(mesh):
    return jax.shard_map(
        body,
        mesh=mesh,
        in_specs=(
            P("col", None, "row", None),
            P(),
            P(("row", "col"), None, None),
            P(("row", "col"), None, None),
            P(("row", "col"), None, None, None, None),
            P(("row", "col"), None, None, None),
        ),
        out_specs=P(None, "row", "col"),
        check_vma=False,
    )
```

time: 839 us -> 107 us (0.13)
  local copies, waits for them, and re-layouts: 272 us -> 1.6 us
  other arithmetic: 266 us -> 0 us
  waiting for transfers between devices: 229 us -> 0 us
  Pallas kernels: 0 us -> 104 us
  matrix products: 27.2 us -> 0 us
  starting transfers between devices: 19 us -> 0 us
  between operations: 16.1 us -> 0.01 us
    gather x12 -> x0, local copies, waits for them, and re-layouts: 204 us -> none  [the longest x6 140 us: tile_step(): jnp.take(by_component, tile_links.reshape(-1), axis=1)]
    psum x1 -> x0, waiting for transfers between devices: 161 us -> none  [body(): summed = lax.psum(combined[:, direction, :], ('row', 'col'))]
    mul x97 -> x0, other arithmetic: 109 us -> none  [the longest x96 108 us: pair_step(): w_pair[:, :, comp, :, None] * moved[comp].astype(jnp.float32)[None, None]]
    pallas_call x0 -> x1, Pallas kernels: none -> 104 us  [body(): pl.pallas_call(kernel, out_shape=jax.ShapeDtypeStruct((3, 64, 32), F32),...]
    add x96 -> x0, other arithmetic: 87.8 us -> none  [pair_step(): pair_sum + w_pair[:, :, comp, :, None] * moved[comp].astype(jnp.float32)[...]
    all_to_all x1 -> x0, waiting for transfers between devices: 68.4 us -> none  [body(): lax.all_to_all(outgoing, ('row', 'col'), split_axis=0, concat_axis=0, til...]
    select_n x16 -> x0, other arithmetic: 52.8 us -> none  [the longest x12 47.1 us: tile_step(): jnp.take(by_component, tile_links.reshape(-1), axis=1)]
    reshape x3 -> x0, local copies, waits for them, and re-layouts: 29.9 us -> none  [the longest x2 17.1 us: body(): arrived.transpose(0, 4, 3, 1, 2).reshape(row_count * slot_len, width)]
  transfers between devices with their start and end apart: 4 -> 0, of which waited for: 2 -> 0; matrix products, arithmetic and copies ran while one was open for 2% -> 0% of each run, Pallas kernels for 0% -> 0%
where the time goes in v1:
time: 107 us; the launch traced here: 106 us
  Pallas kernels  104 us (97%)
  local copies, waits for them, and re-layouts  1.6 us (1%)
    pallas_call x1, Pallas kernels, body(): pl.pallas_call(kernel, out_shape=jax.ShapeDtypeStruct((3, 64, 32), F32),...  104 us

profile of v1, /device:TPU:0, one launch (start us, length us, event | category | flops | bytes accessed | tf_op | source)
XLA Modules:
  0.0 106.0 jit_solution(2785978193731364806)
XLA Ops:
  0.0 104.4 %shard_map.64 = f32[3,64,32]{2,1,0:T(8,128)} custom-call(bf16[3,32,8192]{2,1,0:T(8,128)(2,1)} %bitcast.9, s32[128]{0:T(128)} %sizes.1, s32[2,128]{1,0:T(2,128)} %bitcast.13, s32[16,768]{1,0:T(8,128)} %bitcast.12, f32[144,768]{1,0:T(8,128)} %bitcast.10, f32[48,768]{1,0:T(8,128)} %bitcast.11), custom_call_target="tpu_custom_call" | custom-call | tf_op jit(solution)/shard_map/pallas_call | solution.py:491
  104.4 1.6 %copy.8 = f32[3,64,32]{1,2,0:T(8,128)} copy(f32[3,64,32]{2,1,0:T(8,128)} %shard_map.64) | data formatting | bytes 49152 | tf_op jit(solution)/shard_map/pallas_call | solution.py:491

commit v2 on v1

--- a/solution.py
+++ b/solution.py
@@ -19,7 +19,8 @@
 WROWS = 40
 PITCH = 520
 WHALF = LANE * WROWS
-UNROLL = 8
+UNROLL = 32
+STEP = 5
 FROM_PREV = 1024
 OWN_AFTER = 1152
 OWN_BEFORE = 1280
@@ -32,11 +33,10 @@
     panel, sizes, ghosts, nbrs, force, bond, out,
     modes, table, t32, raw_f, raw_b, raw_n, raw_g, merged, merged_n,
     idx_v, idx_s, ghost_s, u32, weights, pulled, to_next, to_prev, gin,
-    vkeep, vsend, vrecv, part1, send1, recv1, part2, recv2, part3, recv3, fin, fin_in,
+    vkeep, vsend, vrecv, part1, send1, recv1, part2, recv2, part3, recv3,
     local_sem, raw_send, raw_recv, panel_send, panel_recv, fwd_send, fwd_recv,
     ghost_send_sem, ghost_recv_sem, gfwd_send, gfwd_recv,
     core_send, core_recv, s1_send, s1_recv, s2_send, s2_recv, s3_send, s3_recv,
-    fin_send, fin_recv,
 ):
     r = lax.axis_index("row")
     c = lax.axis_index("col")
@@ -62,8 +62,6 @@
 
     barrier = pltpu.get_barrier_semaphore()
     pl.semaphore_signal(barrier, inc=1, device_id=sib, device_id_type=MESH)
-    across = (r, cp * 2 + 1 - s + 2 - 4 * zl)
-    pl.semaphore_signal(barrier, inc=1, device_id=across, device_id_type=MESH)
 
     def greet(i, carry):
         k = lax.rem(me + i, CHIPS)
@@ -84,23 +82,7 @@
     )
     for copy in own:
         copy.start()
-    zero8 = jnp.zeros((8, LANE), F32)
-
-    def clear_w(i, carry):
-        pulled[pl.ds(i * 8, 8), :] = zero8
-        return carry
-
-    lax.fori_loop(0, 2 * WHALF // 8, clear_w, 0)
-
-    def clear_t(i, carry):
-        t32[pl.ds(i * 8, 8), :] = zero8
-        return carry
-
-    lax.fori_loop(0, LANE * 16 // 8, clear_t, 0)
-    for i in range(32):
-        u32[pl.ds(i * 8, 8), :] = zero8
-    table[pl.ds(ZERO_ROW, TABLE - ZERO_ROW)] = jnp.zeros((TABLE - ZERO_ROW, 16, LANE), BF16)
-    pl.semaphore_wait(barrier, CHIPS + 1)
+    pl.semaphore_wait(barrier, CHIPS)
 
     raw_copies = [
         remote(src, dst.at[s], raw_send.at[n], raw_recv.at[n], sib)
@@ -110,7 +92,7 @@
         copy.start()
 
     def panel_copy(i):
-        k = lax.rem(me + i, CHIPS)
+        k = lax.rem(me + i * STEP, CHIPS)
         return remote(
             panel.at[:, :, lanes_of(k)], modes.at[:, cp, s, :, lanes_of(r)],
             panel_send.at[i], panel_recv.at[me], chip_device(k),
@@ -121,6 +103,22 @@
         return carry
 
     lax.fori_loop(1, CHIPS, panel_start, 0)
+    zero8 = jnp.zeros((8, LANE), F32)
+
+    def clear_w(i, carry):
+        pulled[pl.ds(i * 8, 8), :] = zero8
+        return carry
+
+    lax.fori_loop(0, 2 * WHALF // 8, clear_w, 0)
+
+    def clear_t(i, carry):
+        t32[pl.ds(i * 8, 8), :] = zero8
+        return carry
+
+    lax.fori_loop(0, LANE * 16 // 8, clear_t, 0)
+    for i in range(32):
+        u32[pl.ds(i * 8, 8), :] = zero8
+    table[pl.ds(ZERO_ROW, TABLE - ZERO_ROW)] = jnp.zeros((TABLE - ZERO_ROW, 16, LANE), BF16)
     for copy in own:
         copy.wait()
     for copy in raw_copies:
@@ -162,7 +160,8 @@
         inner = v + jnp.where(late, n0, 0)
         outer = v + jnp.where(late, 512, 256)
         row = jnp.where(v < CAP, inner, jnp.where(v >= CHIP_ATOMS, ZERO_ROW, outer))
-        idx_v[:, pl.ds(b * LANE, LANE)] = row
+        wide = jnp.concatenate([row, jnp.zeros((LANE - NBR, LANE), jnp.int32)], axis=0)
+        idx_v[pl.ds(b * LANE, LANE), :] = wide.T
     idx_copy = pltpu.make_async_copy(idx_v, idx_s, local_sem.at[1])
     idx_copy.start()
 
@@ -252,19 +251,44 @@
     lax.fori_loop(1, 8, group, 0)
     build(7)
 
-    def pick(g, carry):
-        gg = s * 64 + g
-        to_next[g] = table[n0 + ghost_s[1, 0, gg]]
-        to_prev[g] = table[ghost_s[0, 1, gg]]
-        return carry
-
-    lax.fori_loop(0, 64, pick, 0, unroll=8)
+    three = lax.broadcasted_iota(jnp.int32, (48, 64), 0)
+    four = lax.broadcasted_iota(jnp.int32, (48, 64), 1)
+    part_of = three // 16
+    kept = (part_of * 16 + lax.rem(three, 16) == four) & (lax.rem(three, 16) < 12)
+    moved = (48 + part_of * 4 + lax.rem(three, 16) - 12 == four) & (lax.rem(three, 16) >= 12)
+    shut = jnp.where(kept | moved, 1.0, 0.0)
+    open_up = shut.T.astype(BF16)
+    shut = shut.astype(BF16)
+
+    def pack_rows(rows):
+        return jnp.dot(shut, jnp.concatenate(rows, axis=0), preferred_element_type=F32).astype(BF16)
+
     nxt = chip_device(lax.rem(me + 1, CHIPS))
     prv = chip_device(lax.rem(me + CHIPS - 1, CHIPS))
-    g_next = remote(to_next, gin.at[0, s], ghost_send_sem.at[0], ghost_recv_sem.at[0], nxt)
-    g_prev = remote(to_prev, gin.at[1, s], ghost_send_sem.at[1], ghost_recv_sem.at[1], prv)
-    g_next.start()
-    g_prev.start()
+
+    def ghost_copy_of(n, h):
+        piece = pl.ds(h * 8, 8)
+        return remote(
+            (to_next, to_prev)[n].at[piece], gin.at[n, s, piece],
+            ghost_send_sem.at[n, h], ghost_recv_sem.at[n, h], (nxt, prv)[n],
+        )
+
+    def share_copy_of(n, h, half):
+        piece = gin.at[n, half, pl.ds(h * 8, 8)]
+        return remote(piece, piece, gfwd_send.at[n, h], gfwd_recv.at[n, h], sib)
+
+    pieces = [(n, h) for h in range(2) for n in range(2)]
+
+    def pick(g, carry):
+        g0 = s * 64 + g * 4
+        to_next[g] = pack_rows([table[n0 + ghost_s[1, 0, g0 + u]] for u in range(4)])
+        to_prev[g] = pack_rows([table[ghost_s[0, 1, g0 + u]] for u in range(4)])
+        return carry
+
+    for h in range(2):
+        lax.fori_loop(h * 8, h * 8 + 8, pick, 0, unroll=8)
+        for n in range(2):
+            ghost_copy_of(n, h).start()
 
     def pick_own(g, carry):
         table[OWN_AFTER + g] = table[n0 + ghost_s[1, 1, g]]
@@ -272,20 +296,24 @@
         return carry
 
     lax.fori_loop(0, GHOST, pick_own, 0, unroll=8)
-    shares = [
-        remote(gin.at[n, s], gin.at[n, s], gfwd_send.at[n], gfwd_recv.at[n], sib) for n in range(2)
-    ]
-    g_next.wait_recv()
-    shares[0].start()
-    g_prev.wait_recv()
-    shares[1].start()
-    for n, base in ((0, FROM_PREV), (1, FROM_NEXT)):
-        table[pl.ds(base + s * 64, 64)] = gin[n, s]
-    for n, base in ((0, FROM_PREV), (1, FROM_NEXT)):
-        remote(
-            gin.at[n, 1 - s], gin.at[n, 1 - s], gfwd_send.at[n], gfwd_recv.at[n], sib
-        ).wait_recv()
-        table[pl.ds(base + (1 - s) * 64, 64)] = gin[n, 1 - s]
+
+    def unpack(n, h, half):
+        base = (FROM_PREV, FROM_NEXT)[n] + half * 64 + h * 32
+
+        def step(g, carry):
+            rows = jnp.dot(open_up, gin[n, half, h * 8 + g], preferred_element_type=F32)
+            table[pl.ds(base + g * 4, 4)] = rows.astype(BF16).reshape(4, 16, LANE)
+            return carry
+
+        lax.fori_loop(0, 8, step, 0, unroll=8)
+
+    for n, h in pieces:
+        ghost_copy_of(n, h).wait_recv()
+        share_copy_of(n, h, s).start()
+        unpack(n, h, s)
+    for n, h in pieces:
+        share_copy_of(n, h, 1 - s).wait_recv()
+        unpack(n, h, 1 - s)
 
     def pull(n, carry):
         i0 = n * UNROLL
@@ -293,7 +321,7 @@
         t0 = lax.rem(i0, LANE)
         q0 = (t0 // 32) * LANE + b * 32 + lax.rem(t0, 32)
         taken = [
-            jnp.concatenate([table[idx_s[j, i0 + u]] for j in range(NBR)], axis=0)
+            jnp.concatenate([table[idx_s[i0 + u, j]] for j in range(NBR)], axis=0)
             for u in range(UNROLL)
         ]
         sums = [
@@ -318,6 +346,10 @@
         return ((j // 2) * 4 + y, (x * 2 + lax.rem(j, 2)) * 2 + s)
 
     my_lanes = pl.ds(pl.multiple_of(s * HALF, HALF), HALF)
+
+    lane_group = lax.broadcasted_iota(jnp.int32, (16, LANE), 1) // 32
+    low = lane_group < 2
+    even = lax.rem(lane_group, 2) == 0
 
     def velocity(a):
         def part(n, carry):
@@ -337,16 +369,27 @@
                 term = jnp.dot(lhs, rhs, preferred_element_type=F32)
                 acc = term if acc is None else acc + term
             for yy in range(4):
-                for ss in range(2):
-                    for ll in range(2):
-                        for xx in range(2):
-                            at = (yy * 4 + ss * 2 + ll) * 16
-                            block = acc[at : at + 16, xx * LANE : xx * LANE + LANE]
-                            pos = {"x": 2 * xp + xx, "y": yy, "z": 2 * zz + ll}
-                            p, q, t = (pos[axis] for axis in orders[a])
-                            place = (p * 4 + q) * 4 + t
-                            vkeep[a, ss, place] = block
-                            vsend[a, ss, place] = block.astype(BF16)
+                for xx in range(2):
+                    at = yy * 64
+                    rows = [
+                        acc[at + 16 * g : at + 16 * g + 16, xx * LANE : xx * LANE + LANE]
+                        for g in range(4)
+                    ]
+                    halves = [None] * 4
+                    for g in range(2):
+                        halves[g] = jnp.where(low, rows[g], pltpu.roll(rows[g + 2], 64, 1))
+                        halves[g + 2] = jnp.where(low, pltpu.roll(rows[g], 64, 1), rows[g + 2])
+                    quarters = [None] * 4
+                    for g in (0, 2):
+                        quarters[g] = jnp.where(even, halves[g], pltpu.roll(halves[g + 1], 32, 1))
+                        quarters[g + 1] = jnp.where(even, pltpu.roll(halves[g], 96, 1), halves[g + 1])
+                    for quarter, block in enumerate(quarters):
+                        ll, ss = divmod(quarter, 2)
+                        pos = {"x": 2 * xp + xx, "y": yy, "z": 2 * zz + ll}
+                        p, q, t = (pos[axis] for axis in orders[a])
+                        place = (p * 4 + q) * 4 + t
+                        vkeep[a, ss, place] = block
+                        vsend[a, ss, place] = block.astype(BF16)
             return carry
 
         lax.fori_loop(0, 4, part, 0)
@@ -419,7 +462,8 @@
     def add4(a):
         mine = where[orders[a][2]]
         total = part3[a, pl.ds(mine, 1)] + stage_wait(a, 2, recv3, s3_recv)
-        fin[a] = total[0]
+        for g in range(4):
+            out[a, pl.ds(g * 16, 16), :] = total[0][:, g * 32 : g * 32 + 32]
 
     velocity(0)
     core_copy(0).start()
@@ -437,29 +481,6 @@
     for a in range(3):
         add4(a)
 
-    slot = s * 2 + zl
-    partners = ((0, 1), (1, 0), (1, 1))
-
-    def partner(dz, ds):
-        zz = jnp.where(dz == 1, 1 - zl, zl) if dz else zl
-        ss = 1 - s if ds else s
-        return (r, (x * 2 + zz) * 2 + ss), ss * 2 + zz
-
-    fin_copies = []
-    for n, (dz, ds) in enumerate(partners):
-        dev, _ = partner(dz, ds)
-        fin_copies.append(remote(fin, fin_in.at[slot], fin_send.at[n], fin_recv.at[slot], dev))
-    for copy in fin_copies:
-        copy.start()
-    fin_in[slot] = fin[...]
-    for dz, ds in partners:
-        _, there = partner(dz, ds)
-        remote(fin, fin_in.at[there], fin_recv.at[there], fin_recv.at[there], sib).wait_recv()
-    shift = lax.rem(LANE - 32 * lax.rem(c, 4), LANE)
-    for a in range(3):
-        for n in range(4):
-            out[a, pl.ds(n * 16, 16), :] = pltpu.roll(fin_in[n, a], shift, 1)[:, :32]
-
     def panel_done(i, carry):
         panel_copy(i).wait_send()
         return carry
@@ -471,16 +492,13 @@
         return carry
 
     lax.fori_loop(0, 8, forward_done, 0)
-    g_next.wait_send()
-    g_prev.wait_send()
-    for copy in shares:
-        copy.wait_send()
+    for n, h in pieces:
+        ghost_copy_of(n, h).wait_send()
+        share_copy_of(n, h, s).wait_send()
     for a in range(3):
         core_copy(a).wait_send()
         for copy in copies1(a) + copies2(a) + copies3(a):
             copy.wait_send()
-    for copy in fin_copies:
-        copy.wait_send()
 
 
 def body(mode_panel, domain_sizes, ghost_send, neighbours, force_blocks, bond_vectors):
@@ -503,15 +521,15 @@
             vm((2, 2, GHOST), jnp.int32),
             vm((192, CHIP_ATOMS), F32),
             vm((NBR, CHIP_ATOMS), jnp.int32),
-            vm((NBR, HALF), jnp.int32),
-            pltpu.SMEM((NBR, HALF), jnp.int32),
+            vm((HALF, LANE), jnp.int32),
+            pltpu.SMEM((HALF, LANE), jnp.int32),
             pltpu.SMEM((2, 2, GHOST), jnp.int32),
             vm((256, LANE), F32),
             vm((HALF, 2 * WROWS, 256), BF16),
             vm((40 * PITCH, LANE), F32),
-            vm((64, 16, LANE), BF16),
-            vm((64, 16, LANE), BF16),
-            vm((2, 2, 64, 16, LANE), BF16),
+            vm((16, 48, LANE), BF16),
+            vm((16, 48, LANE), BF16),
+            vm((2, 2, 16, 48, LANE), BF16),
             vm((3, 2, 64, 16, LANE), F32),
             vm((3, 2, 64, 16, LANE), BF16),
             vm((3, 64, 16, LANE), BF16),
@@ -522,13 +540,10 @@
             vm((3, 4, 4, 16, LANE), F32),
             vm((3, 4, 16, LANE), F32),
             vm((3, 4, 1, 16, LANE), F32),
-            vm((3, 16, LANE), F32),
-            vm((4, 3, 16, LANE), F32),
-            dma((5,)), dma((4,)), dma((4,)), dma((CHIPS,)), dma((CHIPS,)), dma((8,)), dma((8,)),
-            dma((2,)), dma((2,)), dma((2,)), dma((2,)),
+            dma((5,)), dma((4,)), dma((4,)), dma((CHIPS,)), dma((CHIPS,)), dma((CHIPS,)), dma((CHIPS,)),
+            dma((2, 2)), dma((2, 2)), dma((2, 2)), dma((2, 2)),
             dma((3,)), dma((3,)),
             dma((3, 3)), dma((3, 4)), dma((3, 3)), dma((3, 4)), dma((3, 3)), dma((3, 4)),
-            dma((3,)), dma((4,)),
         ],
         compiler_params=pltpu.CompilerParams(
             collective_id=1, has_side_effects=True, vmem_limit_bytes=63 * 2**20

time: 107 us -> 90.4 us (0.84)
  Pallas kernels: 104 us -> 88.6 us
    pallas_call x1, Pallas kernels: 104 us -> 88.6 us  [body(): pl.pallas_call(kernel, out_shape=jax.ShapeDtypeStruct((3, 64, 32), F32),...]
where the time goes in v2:
time: 90.4 us; the launch traced here: 90.2 us
  Pallas kernels  88.6 us (98%)
  local copies, waits for them, and re-layouts  1.6 us (2%)
    pallas_call x1, Pallas kernels, body(): pl.pallas_call(kernel, out_shape=jax.ShapeDtypeStruct((3, 64, 32), F32),...  88.6 us

profile of v2, /device:TPU:0, one launch (start us, length us, event | category | flops | bytes accessed | tf_op | source)
XLA Modules:
  0.0 90.2 jit_solution(8340122344781397226)
XLA Ops:
  0.0 88.6 %shard_map.64 = f32[3,64,32]{2,1,0:T(8,128)} custom-call(bf16[3,32,8192]{2,1,0:T(8,128)(2,1)} %bitcast.9, s32[128]{0:T(128)} %sizes.1, s32[2,128]{1,0:T(2,128)} %bitcast.13, s32[16,768]{1,0:T(8,128)} %bitcast.12, f32[144,768]{1,0:T(8,128)} %bitcast.10, f32[48,768]{1,0:T(8,128)} %bitcast.11), custom_call_target="tpu_custom_call" | custom-call | tf_op jit(solution)/shard_map/pallas_call | solution.py:509
  88.6 1.6 %copy.8 = f32[3,64,32]{1,2,0:T(8,128)} copy(f32[3,64,32]{2,1,0:T(8,128)} %shard_map.64) | data formatting | bytes 49152 | tf_op jit(solution)/shard_map/pallas_call | solution.py:509

commit v3 on v2

--- a/solution.py
+++ b/solution.py
@@ -31,8 +31,8 @@
 
 def kernel(
     panel, sizes, ghosts, nbrs, force, bond, out,
-    modes, table, t32, raw_f, raw_b, raw_n, raw_g, merged, merged_n,
-    idx_v, idx_s, ghost_s, u32, weights, pulled, to_next, to_prev, gin,
+    modes, table, wide, raw_f, raw_b, raw_n, raw_g, merged, merged_n,
+    idx_v, idx_a, idx_b, ghost_s, u32, weights, pulled, to_next, to_prev, gin,
     vkeep, vsend, vrecv, part1, send1, recv1, part2, recv2, part3, recv3,
     local_sem, raw_send, raw_recv, panel_send, panel_recv, fwd_send, fwd_recv,
     ghost_send_sem, ghost_recv_sem, gfwd_send, gfwd_recv,
@@ -111,11 +111,6 @@
 
     lax.fori_loop(0, 2 * WHALF // 8, clear_w, 0)
 
-    def clear_t(i, carry):
-        t32[pl.ds(i * 8, 8), :] = zero8
-        return carry
-
-    lax.fori_loop(0, LANE * 16 // 8, clear_t, 0)
     for i in range(32):
         u32[pl.ds(i * 8, 8), :] = zero8
     table[pl.ds(ZERO_ROW, TABLE - ZERO_ROW)] = jnp.zeros((TABLE - ZERO_ROW, 16, LANE), BF16)
@@ -160,10 +155,8 @@
         inner = v + jnp.where(late, n0, 0)
         outer = v + jnp.where(late, 512, 256)
         row = jnp.where(v < CAP, inner, jnp.where(v >= CHIP_ATOMS, ZERO_ROW, outer))
-        wide = jnp.concatenate([row, jnp.zeros((LANE - NBR, LANE), jnp.int32)], axis=0)
-        idx_v[pl.ds(b * LANE, LANE), :] = wide.T
-    idx_copy = pltpu.make_async_copy(idx_v, idx_s, local_sem.at[1])
-    idx_copy.start()
+        square = jnp.concatenate([row, jnp.zeros((LANE - NBR, LANE), jnp.int32)], axis=0)
+        idx_v[pl.ds(b * LANE, LANE), :] = square.T
 
     block_lane = lax.rem(lax.broadcasted_iota(jnp.int32, (LANE, LANE), 1), 4)
 
@@ -202,17 +195,35 @@
 
     lax.fori_loop(0, 4, weights_block, 0)
     ghost_copy.wait()
-    idx_copy.wait()
+
+    def index_copy(n, slot):
+        return pltpu.make_async_copy(
+            idx_v.at[pl.ds(pl.multiple_of(n * UNROLL, UNROLL), UNROLL)],
+            (idx_a, idx_b)[slot], local_sem.at[slot],
+        )
+
+    def clear_rows(i, carry):
+        wide[i, pl.ds(12, 4), :] = jnp.zeros((4, LANE), F32)
+        return carry
+
+    lax.fori_loop(0, CHIP_ATOMS, clear_rows, 0, unroll=8)
+
+    def half_group(rr, core):
+        return modes.at[:, :, core, :, lanes_of(rr)]
 
     def forward_copy(rr):
-        half = modes.at[:, :, s, :, lanes_of(rr)]
-        return remote(half, half, fwd_send.at[rr], fwd_recv.at[rr], sib)
-
-    def other_copy(rr):
-        half = modes.at[:, :, 1 - s, :, lanes_of(rr)]
-        return remote(half, half, fwd_send.at[rr], fwd_recv.at[rr], sib)
-
-    def arrive(i):
+        return remote(half_group(rr, s), half_group(rr, s), fwd_send.at[rr], fwd_recv.at[rr], sib)
+
+    def build(rr, core):
+        for e in range(3):
+            for xh in range(2):
+                v = modes[e, 4 * xh : 4 * xh + 4, core, :, lanes_of(rr)]
+                vt = v.reshape(LANE, LANE).astype(F32).T
+                for g in range(16):
+                    at = rr * 32 + (g // 4) * 256 + (g % 4) * 8
+                    wide[pl.ds(at, 8), e * 4 + xh + 2 * core, :] = vt[g * 8 : g * 8 + 8]
+
+    def arrive(i, carry):
         rr = lax.rem(r + 7 - i, 8)
 
         def wait_one(cc, carry):
@@ -227,41 +238,30 @@
 
         lax.fori_loop(0, 8, wait_one, 0)
         forward_copy(rr).start()
-
-    def build(i):
-        rr = lax.rem(r + 7 - i, 8)
-        other_copy(rr).wait_recv()
-        for e in range(3):
-            for xx in range(4):
-                v = modes[e, 2 * xx : 2 * xx + 2, :, :, lanes_of(rr)]
-                vt = v.reshape(LANE, LANE).astype(F32).T
-                for g in range(16):
-                    t32[pl.ds(g * 128 + e * 4 + xx, 8, stride=16), :] = vt[g * 8 : g * 8 + 8]
-        for b in range(4):
-            rows = t32[pl.ds(b * 512, 512), :].astype(BF16).reshape(32, 16, LANE)
-            table[pl.ds(b * 256 + rr * 32, 32)] = rows
-
-    arrive(0)
-
-    def group(i, carry):
-        arrive(i)
-        build(i - 1)
-        return carry
-
-    lax.fori_loop(1, 8, group, 0)
-    build(7)
-
-    three = lax.broadcasted_iota(jnp.int32, (48, 64), 0)
-    four = lax.broadcasted_iota(jnp.int32, (48, 64), 1)
-    part_of = three // 16
-    kept = (part_of * 16 + lax.rem(three, 16) == four) & (lax.rem(three, 16) < 12)
-    moved = (48 + part_of * 4 + lax.rem(three, 16) - 12 == four) & (lax.rem(three, 16) >= 12)
-    shut = jnp.where(kept | moved, 1.0, 0.0)
-    open_up = shut.T.astype(BF16)
-    shut = shut.astype(BF16)
-
-    def pack_rows(rows):
-        return jnp.dot(shut, jnp.concatenate(rows, axis=0), preferred_element_type=F32).astype(BF16)
+        build(rr, s)
+        return carry
+
+    lax.fori_loop(0, 8, arrive, 0)
+
+    index_copy(0, 0).start()
+    index_copy(1, 1).start()
+
+    down = lax.broadcasted_iota(jnp.int32, (48, LANE), 0)
+    across = lax.broadcasted_iota(jnp.int32, (48, LANE), 1)
+    six = lax.rem(down, 6)
+    place48 = (down // 6) * 16 + (six // 2) * 4 + lax.rem(six, 2) + 2 * s
+    shut = jnp.where(place48 == across, 1.0, 0.0).astype(BF16)
+    down = lax.broadcasted_iota(jnp.int32, (LANE, 96), 0)
+    across = lax.broadcasted_iota(jnp.int32, (LANE, 96), 1)
+    six = lax.rem(across, 6)
+    core_at = jnp.where(across < 48, s, 1 - s)
+    place96 = (lax.rem(across, 48) // 6) * 16 + (six // 2) * 4 + lax.rem(six, 2) + 2 * core_at
+    open_up = jnp.where(place96 == down, 1.0, 0.0).astype(BF16)
+
+    def pack_rows(atoms):
+        rows = [wide[at] for at in atoms]
+        stacked = jnp.concatenate(rows, axis=0).astype(BF16)
+        return jnp.dot(shut, stacked, preferred_element_type=F32).astype(BF16)
 
     nxt = chip_device(lax.rem(me + 1, CHIPS))
     prv = chip_device(lax.rem(me + CHIPS - 1, CHIPS))
@@ -280,15 +280,25 @@
     pieces = [(n, h) for h in range(2) for n in range(2)]
 
     def pick(g, carry):
-        g0 = s * 64 + g * 4
-        to_next[g] = pack_rows([table[n0 + ghost_s[1, 0, g0 + u]] for u in range(4)])
-        to_prev[g] = pack_rows([table[ghost_s[0, 1, g0 + u]] for u in range(4)])
+        to_next[g] = pack_rows([n0 + ghost_s[1, 0, g * 8 + u] for u in range(8)])
+        to_prev[g] = pack_rows([ghost_s[0, 1, g * 8 + u] for u in range(8)])
         return carry
 
     for h in range(2):
-        lax.fori_loop(h * 8, h * 8 + 8, pick, 0, unroll=8)
+        lax.fori_loop(h * 8, h * 8 + 8, pick, 0, unroll=4)
         for n in range(2):
             ghost_copy_of(n, h).start()
+
+    def finish(rr, carry):
+        other = half_group(rr, 1 - s)
+        remote(other, other, fwd_send.at[rr], fwd_recv.at[rr], sib).wait_recv()
+        build(rr, 1 - s)
+        for b in range(4):
+            first_atom = pl.multiple_of(b * 256 + rr * 32, 32)
+            table[pl.ds(first_atom, 32)] = wide[pl.ds(first_atom, 32)].astype(BF16)
+        return carry
+
+    lax.fori_loop(0, 8, finish, 0)
 
     def pick_own(g, carry):
         table[OWN_AFTER + g] = table[n0 + ghost_s[1, 1, g]]
@@ -297,31 +307,31 @@
 
     lax.fori_loop(0, GHOST, pick_own, 0, unroll=8)
 
-    def unpack(n, h, half):
-        base = (FROM_PREV, FROM_NEXT)[n] + half * 64 + h * 32
+    def unpack(n, h):
+        base = (FROM_PREV, FROM_NEXT)[n] + h * 64
 
         def step(g, carry):
-            rows = jnp.dot(open_up, gin[n, half, h * 8 + g], preferred_element_type=F32)
-            table[pl.ds(base + g * 4, 4)] = rows.astype(BF16).reshape(4, 16, LANE)
+            both = jnp.concatenate([gin[n, s, h * 8 + g], gin[n, 1 - s, h * 8 + g]], axis=0)
+            rows = jnp.dot(open_up, both, preferred_element_type=F32)
+            table[pl.ds(base + g * 8, 8)] = rows.astype(BF16).reshape(8, 16, LANE)
             return carry
 
-        lax.fori_loop(0, 8, step, 0, unroll=8)
+        lax.fori_loop(0, 8, step, 0, unroll=4)
 
     for n, h in pieces:
         ghost_copy_of(n, h).wait_recv()
         share_copy_of(n, h, s).start()
-        unpack(n, h, s)
     for n, h in pieces:
         share_copy_of(n, h, 1 - s).wait_recv()
-        unpack(n, h, 1 - s)
-
-    def pull(n, carry):
+        unpack(n, h)
+
+    def pull(n, idx_s):
         i0 = n * UNROLL
         b = i0 // LANE
         t0 = lax.rem(i0, LANE)
         q0 = (t0 // 32) * LANE + b * 32 + lax.rem(t0, 32)
         taken = [
-            jnp.concatenate([table[idx_s[i0 + u, j]] for j in range(NBR)], axis=0)
+            jnp.concatenate([table[idx_s[u, j]] for j in range(NBR)], axis=0)
             for u in range(UNROLL)
         ]
         sums = [
@@ -331,9 +341,19 @@
             for g in range(5):
                 total = sums[u][g * 8 : g * 8 + 8] + sums[u][40 + g * 8 : 48 + g * 8]
                 pulled[pl.ds(g * 8 * PITCH + q0 + u, 8, stride=PITCH), :] = total
-        return carry
-
-    lax.fori_loop(0, HALF // UNROLL, pull, 0)
+
+    def pull_two(n, carry):
+        for slot, indices in enumerate((idx_a, idx_b)):
+            index_copy(2 * n + slot, slot).wait()
+            pull(2 * n + slot, indices)
+
+            @pl.when(n + 1 < HALF // UNROLL // 2)
+            def _():
+                index_copy(2 * n + 2 + slot, slot).start()
+
+        return carry
+
+    lax.fori_loop(0, HALF // UNROLL // 2, pull_two, 0)
 
     where = {"x": x, "y": y, "z": z}
     orders = ("xyz", "yzx", "zxy")
@@ -351,23 +371,28 @@
     low = lane_group < 2
     even = lax.rem(lane_group, 2) == 0
 
-    def velocity(a):
-        def part(n, carry):
-            xp = n // 2
-            zz = lax.rem(n, 2)
-            acc = None
-            for comp in range(3):
-                row = (a * 3 + comp) * 4 + 2 * xp
-                rhs = jnp.concatenate(
-                    [
-                        pulled[pl.ds(pl.multiple_of(row * PITCH, 8), HALF), :],
-                        pulled[pl.ds(pl.multiple_of((row + 1) * PITCH, 8), HALF), :],
-                    ],
-                    axis=1,
-                ).astype(BF16)
-                lhs = modes[comp, pl.ds(zz * 4, 4), :, :, my_lanes].reshape(256, HALF)
-                term = jnp.dot(lhs, rhs, preferred_element_type=F32)
-                acc = term if acc is None else acc + term
+    def velocity(a, core, keep):
+        def part(zz, carry):
+            rows = [
+                pl.ds(pl.multiple_of(((a * 3 + comp) * 4 + 2 * core + xx) * PITCH, 8), HALF)
+                for comp in range(3)
+                for xx in range(2)
+            ]
+            rhs = jnp.concatenate(
+                [
+                    jnp.concatenate([pulled[rows[2 * comp], :], pulled[rows[2 * comp + 1], :]], axis=1)
+                    for comp in range(3)
+                ],
+                axis=0,
+            ).astype(BF16)
+            lhs = jnp.concatenate(
+                [
+                    modes[comp, pl.ds(zz * 4, 4), :, :, my_lanes].reshape(256, HALF)
+                    for comp in range(3)
+                ],
+                axis=1,
+            )
+            acc = jnp.dot(lhs, rhs, preferred_element_type=F32)
             for yy in range(4):
                 for xx in range(2):
                     at = yy * 64
@@ -384,18 +409,20 @@
                         quarters[g] = jnp.where(even, halves[g], pltpu.roll(halves[g + 1], 32, 1))
                         quarters[g + 1] = jnp.where(even, pltpu.roll(halves[g], 96, 1), halves[g + 1])
                     for quarter, block in enumerate(quarters):
-                        ll, ss = divmod(quarter, 2)
-                        pos = {"x": 2 * xp + xx, "y": yy, "z": 2 * zz + ll}
+                        xl, ll = divmod(quarter, 2)
+                        pos = {"x": 2 * xx + xl, "y": yy, "z": 2 * zz + ll}
                         p, q, t = (pos[axis] for axis in orders[a])
                         place = (p * 4 + q) * 4 + t
-                        vkeep[a, ss, place] = block
-                        vsend[a, ss, place] = block.astype(BF16)
+                        if keep:
+                            vkeep[a, place] = block
+                        else:
+                            vsend[a, place] = block.astype(BF16)
             return carry
 
-        lax.fori_loop(0, 4, part, 0)
+        lax.fori_loop(0, 2, part, 0)
 
     def core_copy(a):
-        return remote(vsend.at[a, 1 - s], vrecv.at[a], core_send.at[a], core_recv.at[a], sib)
+        return remote(vsend.at[a], vrecv.at[a], core_send.at[a], core_recv.at[a], sib)
 
     def stage_copies(a, stage, src, dst, ssem, rsem, size):
         axis = orders[a][stage]
@@ -436,7 +463,7 @@
 
         def step(n, carry):
             at = pl.ds(n * 8, 8)
-            both = vkeep[a, s, at] + vrecv[a, at].astype(F32)
+            both = vkeep[a, at] + vrecv[a, at].astype(F32)
             part1[a, at] = both
             send1[a, at] = both.astype(BF16)
             return carry
@@ -462,17 +489,15 @@
     def add4(a):
         mine = where[orders[a][2]]
         total = part3[a, pl.ds(mine, 1)] + stage_wait(a, 2, recv3, s3_recv)
-        for g in range(4):
-            out[a, pl.ds(g * 16, 16), :] = total[0][:, g * 32 : g * 32 + 32]
-
-    velocity(0)
-    core_copy(0).start()
-    velocity(1)
-    core_copy(1).start()
-    add1(0)
-    velocity(2)
-    core_copy(2).start()
-    add1(1)
+        turned = jnp.concatenate([total[0], jnp.zeros((LANE - 16, LANE), F32)], axis=0).T
+        out[a] = jnp.concatenate([turned[g * 32 : g * 32 + 32, :16] for g in range(4)], axis=1)
+
+    for a in range(3):
+        velocity(a, 1 - s, False)
+        core_copy(a).start()
+        if a:
+            add1(a - 1)
+        velocity(a, s, True)
     add1(2)
     for a in range(3):
         add2(a)
@@ -506,15 +531,15 @@
     any_spec = pl.BlockSpec(memory_space=pl.ANY)
     vm = pltpu.VMEM
     dma = pltpu.SemaphoreType.DMA
-    return pl.pallas_call(
+    turned = pl.pallas_call(
         kernel,
-        out_shape=jax.ShapeDtypeStruct((3, 64, 32), F32),
+        out_shape=jax.ShapeDtypeStruct((3, 32, 64), F32),
         in_specs=[any_spec, pl.BlockSpec(memory_space=pltpu.SMEM)] + [any_spec] * 4,
         out_specs=pl.BlockSpec(memory_space=vm),
         scratch_shapes=[
             vm((3, 8, 2, 32, CHIP_ATOMS), BF16),
             vm((TABLE, 16, LANE), BF16),
-            vm((LANE * 16, LANE), F32),
+            vm((CHIP_ATOMS, 16, LANE), F32),
             vm((2, 144, CAP), F32),
             vm((2, 48, CAP), F32),
             vm((2, NBR, CAP), jnp.int32),
@@ -522,7 +547,8 @@
             vm((192, CHIP_ATOMS), F32),
             vm((NBR, CHIP_ATOMS), jnp.int32),
             vm((HALF, LANE), jnp.int32),
-            pltpu.SMEM((HALF, LANE), jnp.int32),
+            pltpu.SMEM((UNROLL, LANE), jnp.int32),
+            pltpu.SMEM((UNROLL, LANE), jnp.int32),
             pltpu.SMEM((2, 2, GHOST), jnp.int32),
             vm((256, LANE), F32),
             vm((HALF, 2 * WROWS, 256), BF16),
@@ -530,8 +556,8 @@
             vm((16, 48, LANE), BF16),
             vm((16, 48, LANE), BF16),
             vm((2, 2, 16, 48, LANE), BF16),
-            vm((3, 2, 64, 16, LANE), F32),
-            vm((3, 2, 64, 16, LANE), BF16),
+            vm((3, 64, 16, LANE), F32),
+            vm((3, 64, 16, LANE), BF16),
             vm((3, 64, 16, LANE), BF16),
             vm((3, 64, 16, LANE), F32),
             vm((3, 64, 16, LANE), BF16),
@@ -556,6 +582,7 @@
         force_blocks.reshape(144, 768),
         bond_vectors.reshape(48, 768),
     )
+    return turned.transpose(0, 2, 1)
 
 
 def solution(mesh):

time: 90.4 us -> 83.9 us (0.928)
  Pallas kernels: 88.6 us -> 82.3 us
    pallas_call x1, Pallas kernels: 88.6 us -> 82.3 us  [body(): pl.pallas_call(kernel, out_shape=jax.ShapeDtypeStruct((3, 32, 64), F32),...]
    pallas_call x1 -> x0, local copies, waits for them, and re-layouts: 1.6 us -> none  [body(): pl.pallas_call(kernel, out_shape=jax.ShapeDtypeStruct((3, 64, 32), F32),...]
    unnamed x0 -> x1, local copies, waits for them, and re-layouts: none -> 1.42 us
where the time goes in v3:
time: 83.9 us; the launch traced here: 83.7 us
  Pallas kernels  82.3 us (98%)
  local copies, waits for them, and re-layouts  1.42 us (2%)
    pallas_call x1, Pallas kernels, body(): pl.pallas_call(kernel, out_shape=jax.ShapeDtypeStruct((3, 32, 64), F32),...  82.3 us

profile of v3, /device:TPU:0, one launch (start us, length us, event | category | flops | bytes accessed | tf_op | source)
XLA Modules:
  0.0 83.7 jit_solution(2079511458800925911)
XLA Ops:
  0.0 82.3 %shard_map.64 = f32[3,32,64]{2,1,0:T(8,128)} custom-call(bf16[3,32,8192]{2,1,0:T(8,128)(2,1)} %bitcast.10, s32[128]{0:T(128)} %sizes.1, s32[2,128]{1,0:T(2,128)} %bitcast.15, s32[16,768]{1,0:T(8,128)} %bitcast.14, f32[144,768]{1,0:T(8,128)} %bitcast.11, f32[48,768]{1,0:T(8,128)} %bitcast.13), custom_call_target="tpu_custom_call" | custom-call | tf_op jit(solution)/shard_map/pallas_call | solution.py:534
  82.3 1.4 %copy.9 = f32[3,64,32]{1,2,0:T(8,128)} copy(f32[3,64,32]{1,2,0:T(8,128)} %bitcast.12) | data formatting | bytes 49152

commit v4 on v3

--- a/solution.py
+++ b/solution.py
@@ -33,10 +33,10 @@
     panel, sizes, ghosts, nbrs, force, bond, out,
     modes, table, wide, raw_f, raw_b, raw_n, raw_g, merged, merged_n,
     idx_v, idx_a, idx_b, ghost_s, u32, weights, pulled, to_next, to_prev, gin,
-    vkeep, vsend, vrecv, part1, send1, recv1, part2, recv2, part3, recv3,
+    vkeep, vsend, vrecv, part1, send1, recv1, part2, recv2,
     local_sem, raw_send, raw_recv, panel_send, panel_recv, fwd_send, fwd_recv,
     ghost_send_sem, ghost_recv_sem, gfwd_send, gfwd_recv,
-    core_send, core_recv, s1_send, s1_recv, s2_send, s2_recv, s3_send, s3_recv,
+    core_send, core_recv, s1_send, s1_recv, s2_send, s2_recv,
 ):
     r = lax.axis_index("row")
     c = lax.axis_index("col")
@@ -68,7 +68,7 @@
         pl.semaphore_signal(barrier, inc=1, device_id=chip_device(k), device_id_type=MESH)
         return carry
 
-    lax.fori_loop(1, CHIPS, greet, 0)
+    lax.fori_loop(1, CHIPS, greet, 0, unroll=9)
 
     raws = ((force, raw_f), (bond, raw_b), (nbrs, raw_n), (ghosts, raw_g))
     own = [
@@ -102,7 +102,7 @@
         panel_copy(i).start()
         return carry
 
-    lax.fori_loop(1, CHIPS, panel_start, 0)
+    lax.fori_loop(1, CHIPS, panel_start, 0, unroll=7)
     zero8 = jnp.zeros((8, LANE), F32)
 
     def clear_w(i, carry):
@@ -318,6 +318,17 @@
 
         lax.fori_loop(0, 8, step, 0, unroll=4)
 
+    def panel_done(i, carry):
+        panel_copy(i).wait_send()
+        return carry
+
+    lax.fori_loop(1, CHIPS, panel_done, 0, unroll=7)
+
+    def forward_done(i, carry):
+        forward_copy(i).wait_send()
+        return carry
+
+    lax.fori_loop(0, 8, forward_done, 0)
     for n, h in pieces:
         ghost_copy_of(n, h).wait_recv()
         share_copy_of(n, h, s).start()
@@ -387,15 +398,14 @@
             ).astype(BF16)
             lhs = jnp.concatenate(
                 [
-                    modes[comp, pl.ds(zz * 4, 4), :, :, my_lanes].reshape(256, HALF)
+                    modes[comp, :, :, :, my_lanes].reshape(HALF, HALF)
                     for comp in range(3)
                 ],
                 axis=1,
             )
             acc = jnp.dot(lhs, rhs, preferred_element_type=F32)
-            for yy in range(4):
-                for xx in range(2):
-                    at = yy * 64
+            for zz, yy, xx in [(i // 8, i // 2 % 4, i % 2) for i in range(16)]:
+                    at = zz * 256 + yy * 64
                     rows = [
                         acc[at + 16 * g : at + 16 * g + 16, xx * LANE : xx * LANE + LANE]
                         for g in range(4)
@@ -419,7 +429,7 @@
                             vsend[a, place] = block.astype(BF16)
             return carry
 
-        lax.fori_loop(0, 2, part, 0)
+        lax.fori_loop(0, 1, part, 0)
 
     def core_copy(a):
         return remote(vsend.at[a], vrecv.at[a], core_send.at[a], core_recv.at[a], sib)
@@ -452,11 +462,22 @@
     def copies1(a):
         return stage_copies(a, 0, send1, recv1, s1_send, s1_recv, 16)
 
-    def copies2(a):
-        return stage_copies(a, 1, part2, recv2, s2_send, s2_recv, 4)
-
-    def copies3(a):
-        return stage_copies(a, 2, part3, recv3, s3_send, s3_recv, 1)
+    def plane_copy(a, d):
+        first_axis, second_axis = orders[a][1:]
+        mine = where[first_axis] * 4 + where[second_axis]
+        other = lax.rem(mine + d, 16)
+        at = dict(where)
+        at[first_axis] = other // 4
+        at[second_axis] = lax.rem(other, 4)
+        dev = ((at["z"] // 2) * 4 + at["y"], (at["x"] * 2 + lax.rem(at["z"], 2)) * 2 + s)
+        out_copy = remote(
+            part2.at[a, other], recv2.at[a, mine], s2_send.at[a, d], s2_recv.at[a, mine], dev
+        )
+        return out_copy, other
+
+    def plane_wait(a, other):
+        piece = recv2.at[a, other]
+        remote(piece, piece, s2_send.at[a, 0], s2_recv.at[a, other], sib).wait_recv()
 
     def add1(a):
         core_copy(a).wait_recv()
@@ -476,20 +497,23 @@
         mine = where[orders[a][0]]
         total = part1[a, pl.ds(mine * 16, 16)] + stage_wait(a, 0, recv1, s1_recv)
         part2[a] = total
-        for copy in copies2(a):
-            copy.start()
+
+        def send_one(d, carry):
+            plane_copy(a, d)[0].start()
+            return carry
+
+        lax.fori_loop(1, 16, send_one, 0, unroll=5)
 
     def add3(a):
-        mine = where[orders[a][1]]
-        total = part2[a, pl.ds(mine * 4, 4)] + stage_wait(a, 1, recv2, s2_recv)
-        part3[a] = total
-        for copy in copies3(a):
-            copy.start()
-
-    def add4(a):
-        mine = where[orders[a][2]]
-        total = part3[a, pl.ds(mine, 1)] + stage_wait(a, 2, recv3, s3_recv)
-        turned = jnp.concatenate([total[0], jnp.zeros((LANE - 16, LANE), F32)], axis=0).T
+        mine = where[orders[a][1]] * 4 + where[orders[a][2]]
+
+        def take_one(d, total):
+            other = lax.rem(mine + d, 16)
+            plane_wait(a, other)
+            return total + recv2[a, other]
+
+        total = lax.fori_loop(1, 16, take_one, part2[a, mine], unroll=5)
+        turned = jnp.concatenate([total, jnp.zeros((LANE - 16, LANE), F32)], axis=0).T
         out[a] = jnp.concatenate([turned[g * 32 : g * 32 + 32, :16] for g in range(4)], axis=1)
 
     for a in range(3):
@@ -501,29 +525,23 @@
     add1(2)
     for a in range(3):
         add2(a)
-    for a in range(3):
-        add3(a)
-    for a in range(3):
-        add4(a)
-
-    def panel_done(i, carry):
-        panel_copy(i).wait_send()
-        return carry
-
-    lax.fori_loop(1, CHIPS, panel_done, 0)
-
-    def forward_done(i, carry):
-        forward_copy(i).wait_send()
-        return carry
-
-    lax.fori_loop(0, 8, forward_done, 0)
     for n, h in pieces:
         ghost_copy_of(n, h).wait_send()
         share_copy_of(n, h, s).wait_send()
     for a in range(3):
         core_copy(a).wait_send()
-        for copy in copies1(a) + copies2(a) + copies3(a):
+        for copy in copies1(a):
             copy.wait_send()
+    for a in range(3):
+        add3(a)
+
+    for a in range(3):
+
+        def sent_one(d, carry, a=a):
+            plane_copy(a, d)[0].wait_send()
+            return carry
+
+        lax.fori_loop(1, 16, sent_one, 0, unroll=5)
 
 
 def body(mode_panel, domain_sizes, ghost_send, neighbours, force_blocks, bond_vectors):
@@ -563,13 +581,11 @@
             vm((3, 64, 16, LANE), BF16),
             vm((3, 4, 16, 16, LANE), BF16),
             vm((3, 16, 16, LANE), F32),
-            vm((3, 4, 4, 16, LANE), F32),
-            vm((3, 4, 16, LANE), F32),
-            vm((3, 4, 1, 16, LANE), F32),
+            vm((3, 16, 16, LANE), F32),
             dma((5,)), dma((4,)), dma((4,)), dma((CHIPS,)), dma((CHIPS,)), dma((CHIPS,)), dma((CHIPS,)),
             dma((2, 2)), dma((2, 2)), dma((2, 2)), dma((2, 2)),
             dma((3,)), dma((3,)),
-            dma((3, 3)), dma((3, 4)), dma((3, 3)), dma((3, 4)), dma((3, 3)), dma((3, 4)),
+            dma((3, 3)), dma((3, 4)), dma((3, 16)), dma((3, 16)),
         ],
         compiler_params=pltpu.CompilerParams(
             collective_id=1, has_side_effects=True, vmem_limit_bytes=63 * 2**20

time: 83.9 us -> 81 us (0.965)
  Pallas kernels: 82.3 us -> 79.4 us
    pallas_call x1, Pallas kernels: 82.3 us -> 79.4 us  [body(): pl.pallas_call(kernel, out_shape=jax.ShapeDtypeStruct((3, 32, 64), F32),...]
where the time goes in v4:
time: 81 us; the launch traced here: 80.8 us
  Pallas kernels  79.4 us (98%)
  local copies, waits for them, and re-layouts  1.42 us (2%)
    pallas_call x1, Pallas kernels, body(): pl.pallas_call(kernel, out_shape=jax.ShapeDtypeStruct((3, 32, 64), F32),...  79.4 us

profile of v4, /device:TPU:0, one launch (start us, length us, event | category | flops | bytes accessed | tf_op | source)
XLA Modules:
  0.0 80.8 jit_solution(271598028291435777)
XLA Ops:
  0.0 79.4 %shard_map.64 = f32[3,32,64]{2,1,0:T(8,128)} custom-call(bf16[3,32,8192]{2,1,0:T(8,128)(2,1)} %bitcast.10, s32[128]{0:T(128)} %sizes.1, s32[2,128]{1,0:T(2,128)} %bitcast.15, s32[16,768]{1,0:T(8,128)} %bitcast.14, f32[144,768]{1,0:T(8,128)} %bitcast.11, f32[48,768]{1,0:T(8,128)} %bitcast.13), custom_call_target="tpu_custom_call" | custom-call | tf_op jit(solution)/shard_map/pallas_call | solution.py:552
  79.4 1.4 %copy.9 = f32[3,64,32]{1,2,0:T(8,128)} copy(f32[3,64,32]{1,2,0:T(8,128)} %bitcast.12) | data formatting | bytes 49152

commit v5 on v4

--- a/solution.py
+++ b/solution.py
@@ -237,7 +237,6 @@
             return carry
 
         lax.fori_loop(0, 8, wait_one, 0)
-        forward_copy(rr).start()
         build(rr, s)
         return carry
 
@@ -284,10 +283,15 @@
         to_prev[g] = pack_rows([ghost_s[0, 1, g * 8 + u] for u in range(8)])
         return carry
 
+    def forward(rr, carry):
+        forward_copy(rr).start()
+        return carry
+
     for h in range(2):
         lax.fori_loop(h * 8, h * 8 + 8, pick, 0, unroll=4)
         for n in range(2):
             ghost_copy_of(n, h).start()
+        lax.fori_loop(h * 4, h * 4 + 4, forward, 0)
 
     def finish(rr, carry):
         other = half_group(rr, 1 - s)
@@ -482,16 +486,15 @@
     def add1(a):
         core_copy(a).wait_recv()
 
-        def step(n, carry):
-            at = pl.ds(n * 8, 8)
+        copies = copies1(a)
+        mine = where[orders[a][0]]
+        for d in (1, 3, 2, 0):
+            at = pl.ds(lax.rem(mine + d, 4) * 16, 16)
             both = vkeep[a, at] + vrecv[a, at].astype(F32)
             part1[a, at] = both
-            send1[a, at] = both.astype(BF16)
-            return carry
-
-        lax.fori_loop(0, 8, step, 0)
-        for copy in copies1(a):
-            copy.start()
+            if d:
+                send1[a, at] = both.astype(BF16)
+                copies[d - 1].start()
 
     def add2(a):
         mine = where[orders[a][0]]

time: 81 us -> 80.6 us (level)
  no operation moved by 1% of the time
where the time goes in v5:
time: 80.6 us; the launch traced here: 80.5 us
  Pallas kernels  79.1 us (98%)
  local copies, waits for them, and re-layouts  1.42 us (2%)
    pallas_call x1, Pallas kernels, body(): pl.pallas_call(kernel, out_shape=jax.ShapeDtypeStruct((3, 32, 64), F32),...  79.1 us

profile of v5, /device:TPU:0, one launch (start us, length us, event | category | flops | bytes accessed | tf_op | source)
XLA Modules:
  0.0 80.5 jit_solution(9555740602899545638)
XLA Ops:
  0.0 79.1 %shard_map.64 = f32[3,32,64]{2,1,0:T(8,128)} custom-call(bf16[3,32,8192]{2,1,0:T(8,128)(2,1)} %bitcast.10, s32[128]{0:T(128)} %sizes.1, s32[2,128]{1,0:T(2,128)} %bitcast.15, s32[16,768]{1,0:T(8,128)} %bitcast.14, f32[144,768]{1,0:T(8,128)} %bitcast.11, f32[48,768]{1,0:T(8,128)} %bitcast.13), custom_call_target="tpu_custom_call" | custom-call | tf_op jit(solution)/shard_map/pallas_call | solution.py:555
  79.1 1.4 %copy.9 = f32[3,64,32]{1,2,0:T(8,128)} copy(f32[3,64,32]{1,2,0:T(8,128)} %bitcast.12) | data formatting | bytes 49152

commit v6 on v5

--- a/solution.py
+++ b/solution.py
@@ -266,17 +266,17 @@
     prv = chip_device(lax.rem(me + CHIPS - 1, CHIPS))
 
     def ghost_copy_of(n, h):
-        piece = pl.ds(h * 8, 8)
+        piece = pl.ds(h * 4, 4)
         return remote(
             (to_next, to_prev)[n].at[piece], gin.at[n, s, piece],
             ghost_send_sem.at[n, h], ghost_recv_sem.at[n, h], (nxt, prv)[n],
         )
 
     def share_copy_of(n, h, half):
-        piece = gin.at[n, half, pl.ds(h * 8, 8)]
+        piece = gin.at[n, half, pl.ds(h * 4, 4)]
         return remote(piece, piece, gfwd_send.at[n, h], gfwd_recv.at[n, h], sib)
 
-    pieces = [(n, h) for h in range(2) for n in range(2)]
+    pieces = [(n, h) for h in range(4) for n in range(2)]
 
     def pick(g, carry):
         to_next[g] = pack_rows([n0 + ghost_s[1, 0, g * 8 + u] for u in range(8)])
@@ -287,11 +287,11 @@
         forward_copy(rr).start()
         return carry
 
-    for h in range(2):
-        lax.fori_loop(h * 8, h * 8 + 8, pick, 0, unroll=4)
+    for h in range(4):
+        lax.fori_loop(h * 4, h * 4 + 4, pick, 0, unroll=4)
         for n in range(2):
             ghost_copy_of(n, h).start()
-        lax.fori_loop(h * 4, h * 4 + 4, forward, 0)
+        lax.fori_loop(h * 2, h * 2 + 2, forward, 0)
 
     def finish(rr, carry):
         other = half_group(rr, 1 - s)
@@ -312,15 +312,15 @@
     lax.fori_loop(0, GHOST, pick_own, 0, unroll=8)
 
     def unpack(n, h):
-        base = (FROM_PREV, FROM_NEXT)[n] + h * 64
+        base = (FROM_PREV, FROM_NEXT)[n] + h * 32
 
         def step(g, carry):
-            both = jnp.concatenate([gin[n, s, h * 8 + g], gin[n, 1 - s, h * 8 + g]], axis=0)
+            both = jnp.concatenate([gin[n, s, h * 4 + g], gin[n, 1 - s, h * 4 + g]], axis=0)
             rows = jnp.dot(open_up, both, preferred_element_type=F32)
             table[pl.ds(base + g * 8, 8)] = rows.astype(BF16).reshape(8, 16, LANE)
             return carry
 
-        lax.fori_loop(0, 8, step, 0, unroll=4)
+        lax.fori_loop(0, 4, step, 0, unroll=4)
 
     def panel_done(i, carry):
         panel_copy(i).wait_send()
@@ -586,7 +586,7 @@
             vm((3, 16, 16, LANE), F32),
             vm((3, 16, 16, LANE), F32),
             dma((5,)), dma((4,)), dma((4,)), dma((CHIPS,)), dma((CHIPS,)), dma((CHIPS,)), dma((CHIPS,)),
-            dma((2, 2)), dma((2, 2)), dma((2, 2)), dma((2, 2)),
+            dma((2, 4)), dma((2, 4)), dma((2, 4)), dma((2, 4)),
             dma((3,)), dma((3,)),
             dma((3, 3)), dma((3, 4)), dma((3, 16)), dma((3, 16)),
         ],

time: 80.6 us -> 79.7 us (0.989)
  Pallas kernels: 79.1 us -> 78.1 us
    pallas_call x1, Pallas kernels: 79.1 us -> 78.1 us  [body(): pl.pallas_call(kernel, out_shape=jax.ShapeDtypeStruct((3, 32, 64), F32),...]
where the time goes in v6:
time: 79.7 us; the launch traced here: 79.5 us
  Pallas kernels  78.1 us (98%)
  local copies, waits for them, and re-layouts  1.42 us (2%)
    pallas_call x1, Pallas kernels, body(): pl.pallas_call(kernel, out_shape=jax.ShapeDtypeStruct((3, 32, 64), F32),...  78.1 us

profile of v6, /device:TPU:0, one launch (start us, length us, event | category | flops | bytes accessed | tf_op | source)
XLA Modules:
  0.0 79.5 jit_solution(7447901838846715009)
XLA Ops:
  0.0 78.1 %shard_map.64 = f32[3,32,64]{2,1,0:T(8,128)} custom-call(bf16[3,32,8192]{2,1,0:T(8,128)(2,1)} %bitcast.10, s32[128]{0:T(128)} %sizes.1, s32[2,128]{1,0:T(2,128)} %bitcast.15, s32[16,768]{1,0:T(8,128)} %bitcast.14, f32[144,768]{1,0:T(8,128)} %bitcast.11, f32[48,768]{1,0:T(8,128)} %bitcast.13), custom_call_target="tpu_custom_call" | custom-call | tf_op jit(solution)/shard_map/pallas_call | solution.py:555
  78.1 1.4 %copy.9 = f32[3,64,32]{1,2,0:T(8,128)} copy(f32[3,64,32]{1,2,0:T(8,128)} %bitcast.12) | data formatting | bytes 49152
